TPU v7x, 32 devices: a whole 2x2x4 slice. The times are simulated.
32 devices in a mesh: dp: 4 (over y, x), blk: 8 (over z, core).
Axes of the slice: x: 2, y: 2, z: 4, core: 2. Of those that a mesh axis runs over, the one named last changes fastest.
Arguments:
- tokens: bfloat16 [2, 4, 1024, 768], P(None, 'dp', 'blk'), may hold values from -6 to 6
- lengths: int32 [2, 4], P(None, 'dp'), may hold values from 256 to 1024, as said below
- w_query: bfloat16 [768, 768], P('dp'), may hold values from -0.21875 to 0.21875
- w_key: bfloat16 [768, 768], P('dp'), may hold values from -0.21875 to 0.21875
- w_value: bfloat16 [768, 768], P('dp'), may hold values from -0.21875 to 0.21875
- w_output: bfloat16 [768, 768], P('dp'), may hold values from -4 to 4
- w_gate: bfloat16 [768, 3072], P('dp'), may hold values from -0.21875 to 0.21875
- w_up: bfloat16 [768, 3072], P('dp'), may hold values from -0.21875 to 0.21875
- w_down: bfloat16 [3072, 768], P('dp'), may hold values from -0.109375 to 0.109375
- first_gain: bfloat16 [768], P('dp'), may hold values from 0.5 to 1.5
- first_bias: bfloat16 [768], P('dp'), may hold values from -3 to 3
- second_gain: bfloat16 [768], P('dp'), may hold values from 0.5 to 1.5
- second_bias: bfloat16 [768], P('dp'), may hold values from -3 to 3
- cotangent: bfloat16 [2, 4, 1024, 768], P(None, 'dp', 'blk'), may hold values from -6 to 6
Outputs:
- layer_out: bfloat16 [2, 4, 1024, 768], P(None, 'dp', 'blk')
- grad_tokens: float32 [2, 4, 1024, 768], P(None, 'dp', 'blk')
- grad_query: float32 [768, 768], P('dp')
- grad_key: float32 [768, 768], P('dp')
- grad_value: float32 [768, 768], P('dp')
- grad_output: float32 [768, 768], P('dp')
- grad_gate: float32 [768, 3072], P('dp')
- grad_up: float32 [768, 3072], P('dp')
- grad_down: float32 [3072, 768], P('dp')
- grad_first_gain: float32 [768], P('dp')
- grad_first_bias: float32 [768], P('dp')
- grad_second_gain: float32 [768], P('dp')
- grad_second_bias: float32 [768], P('dp')
Inputs may be any that keep to these rules, and one draw needn't show every extreme that they name: `lengths`: each entry is the number of valid leading slots of its sequence. Among the 2 sequences that share an index of dp, at least one has all 1024 slots valid.
All inputs are finite; a program needn't handle non-finite values.
Results may differ from a plain program's by a relative error of at most 0.025.
Values may be sent and summed in bfloat16 or wider, within the bound.
No kernel may reach another device: no remote copies, remote signals or barrier semaphores. Data moves between devices by JAX's collectives and lax.ppermute only.
A program may use at most 256 MiB of HBM per device.

v0:
```python
import math

import jax
import jax.numpy as jnp
from jax import lax
from jax.sharding import PartitionSpec as P

HEAD_DIM = 64


def rotary(positions, head_dim):
    half_dim = head_dim // 2
    frequency = 1000.0 ** (-(jnp.arange(half_dim).astype(jnp.float32) * 2.0 / head_dim))
    angles = positions.astype(jnp.float32)[:, None] * frequency[None, :]
    return (jnp.cos(angles), jnp.sin(angles))


def rotate(values, cosine_table, sine_table):
    half_dim = values.shape[-1] // 2
    first_half = values[..., :half_dim]
    second_half = values[..., half_dim:]
    cosine_b = cosine_table[:, None, :]
    sine_b = sine_table[:, None, :]
    return jnp.concatenate(
        [
            first_half * cosine_b - second_half * sine_b,
            second_half * cosine_b + first_half * sine_b,
        ],
        axis=-1,
    )


def unrotate(values, cosine_table, sine_table):
    half_dim = values.shape[-1] // 2
    first_half = values[..., :half_dim]
    second_half = values[..., half_dim:]
    cosine_b = cosine_table[:, None, :]
    sine_b = sine_table[:, None, :]
    return jnp.concatenate(
        [
            first_half * cosine_b + second_half * sine_b,
            second_half * cosine_b - first_half * sine_b,
        ],
        axis=-1,
    )


def layer_norm(features):
    average = jnp.mean(features, axis=-1, keepdims=True)
    centred = features - average
    variance = jnp.mean(centred * centred, axis=-1, keepdims=True)
    return centred * lax.rsqrt(variance + 1e-05)


def norm_affine(features, gain_vec, bias_vec):
    return layer_norm(features) * gain_vec + bias_vec


def swiglu(gate_in, up_in):
    return jax.nn.silu(gate_in) * up_in


def matmul(left_op, right_op):
    return jnp.dot(left_op, right_op, preferred_element_type=jnp.float32)


def matmul_tn(left_op, right_op):
    return jnp.einsum("nd,nf->df", left_op, right_op, preferred_element_type=jnp.float32)


def matmul_nt(left_op, right_op):
    return jnp.einsum("nf,df->nd", left_op, right_op, preferred_element_type=jnp.float32)


def block_scores(queries, keys_block, valid_block):
    scores = (
        jnp.einsum("snhd,skhd->shnk", queries, keys_block, preferred_element_type=jnp.float32)
        * 0.125
    )
    return jnp.where(valid_block[:, None, None, :], scores, -1e30)


def attention_forward(queries, keys_all, values_all, key_valid):
    seq_count, seq_len = (keys_all.shape[0], keys_all.shape[1])
    block_width = math.gcd(seq_len, 1024)
    blocks = seq_len // block_width

    def slice_block(source, number):
        return lax.dynamic_slice_in_dim(source, number * block_width, block_width, 1)

    def max_pass(number, loop_carry):
        running, totals = loop_carry
        valid_block = slice_block(key_valid, number)
        scores = block_scores(queries, slice_block(keys_all, number), valid_block)
        newest = jnp.maximum(running, jnp.max(scores, axis=-1))
        weights_now = jnp.where(
            valid_block[:, None, None, :], jnp.exp(scores - newest[..., None]), 0.0
        )
        totals = totals * jnp.exp(running - newest) + jnp.sum(weights_now, axis=-1)
        return (newest, totals)

    stat_shape = (seq_count, queries.shape[2], queries.shape[1])
    running, totals = lax.fori_loop(
        0,
        blocks,
        max_pass,
        (jnp.full(stat_shape, -1e30, jnp.float32), jnp.zeros(stat_shape, jnp.float32)),
    )
    log_total = running + jnp.log(totals)

    def value_pass(number, summed):
        valid_block = slice_block(key_valid, number)
        scores = block_scores(queries, slice_block(keys_all, number), valid_block)
        probability = jnp.where(
            valid_block[:, None, None, :], jnp.exp(scores - log_total[..., None]), 0.0
        ).astype(jnp.bfloat16)
        return summed + jnp.einsum(
            "shnk,skhd->snhd",
            probability,
            slice_block(values_all, number),
            preferred_element_type=jnp.float32,
        )

    summed = lax.fori_loop(0, blocks, value_pass, jnp.zeros(queries.shape, jnp.float32))
    return (summed, log_total)


def attention_backward(
    queries, keys_all, values_all, key_valid, grad_attended, log_total, row_delta
):
    seq_count, seq_len, head_count, head_dim = keys_all.shape
    block_width = math.gcd(seq_len, 1024)
    blocks = seq_len // block_width
    model_width = head_count * head_dim

    def slice_block(source, number):
        return lax.dynamic_slice_in_dim(source, number * block_width, block_width, 1)

    def back_pass(number, loop_carry):
        grad_queries, key_terms = loop_carry
        keys_block = slice_block(keys_all, number)
        values_block = slice_block(values_all, number)
        valid_block = slice_block(key_valid, number)
        scores = block_scores(queries, keys_block, valid_block)
        probability = jnp.where(
            valid_block[:, None, None, :], jnp.exp(scores - log_total[..., None]), 0.0
        )
        grad_probs = jnp.einsum(
            "snhd,skhd->shnk", grad_attended, values_block, preferred_element_type=jnp.float32
        )
        grad_scores = (probability * (grad_probs - row_delta[..., None])).astype(jnp.bfloat16)
        grad_queries = (
            grad_queries
            + jnp.einsum(
                "shnk,skhd->snhd", grad_scores, keys_block, preferred_element_type=jnp.float32
            )
            * 0.125
        )
        probs_low = probability.astype(jnp.bfloat16)
        grad_keys = (
            jnp.einsum("shnk,snhd->skhd", grad_scores, queries, preferred_element_type=jnp.float32)
            * 0.125
        )
        grad_values = jnp.einsum(
            "shnk,snhd->skhd", probs_low, grad_attended, preferred_element_type=jnp.float32
        )
        block_terms = jnp.concatenate(
            [
                grad_keys.reshape(seq_count, block_width, model_width),
                grad_values.reshape(seq_count, block_width, model_width),
            ],
            axis=-1,
        )
        key_terms = lax.dynamic_update_slice_in_dim(key_terms, block_terms, number * block_width, 1)
        return (grad_queries, key_terms)

    empty_terms = jnp.zeros((seq_count, seq_len, 2 * model_width), jnp.float32)
    initial = (jnp.zeros(queries.shape, jnp.float32), empty_terms)
    return lax.fori_loop(0, blocks, back_pass, initial)


def shards(
    tokens,
    lengths,
    w_query,
    w_key,
    w_value,
    w_output,
    w_gate,
    w_up,
    w_down,
    first_gain,
    first_bias,
    second_gain,
    second_bias,
    cotangent,
):
    micro_count, seq_count, local_len, model_width = tokens.shape
    cycle_size = lax.axis_size("blk")
    seq_len = local_len * cycle_size
    head_dim = HEAD_DIM
    head_count = model_width // head_dim
    cycle_place = lax.axis_index("blk")
    positions = cycle_place * local_len + jnp.arange(local_len, dtype=jnp.int32)
    cosine_table, sine_table = rotary(positions, head_dim)
    key_slots = jnp.arange(seq_len, dtype=jnp.int32)
    layer_list = []
    grad_list = []
    grad_totals = None

    def split_heads(source):
        return source.reshape(seq_count, local_len, head_count, head_dim)

    for micro_index in range(micro_count):
        (
            full_query,
            full_key,
            full_value,
            full_output,
            full_gate,
            full_up,
            full_down,
            gain_one,
            bias_one,
            gain_two,
            bias_two,
        ) = (
            lax.all_gather(w_query, "dp", axis=0, tiled=True),
            lax.all_gather(w_key, "dp", axis=0, tiled=True),
            lax.all_gather(w_value, "dp", axis=0, tiled=True),
            lax.all_gather(w_output, "dp", axis=0, tiled=True),
            lax.all_gather(w_gate, "dp", axis=0, tiled=True),
            lax.all_gather(w_up, "dp", axis=0, tiled=True),
            lax.all_gather(w_down, "dp", axis=0, tiled=True),
            lax.all_gather(first_gain, "dp", axis=0, tiled=True),
            lax.all_gather(first_bias, "dp", axis=0, tiled=True),
            lax.all_gather(second_gain, "dp", axis=0, tiled=True),
            lax.all_gather(second_bias, "dp", axis=0, tiled=True),
        )
        token_rows = tokens[micro_index].reshape(seq_count * local_len, model_width)
        lengths_now = lengths[micro_index]
        local_valid = positions[None, :] < lengths_now[:, None]
        row_valid = local_valid.reshape(-1)
        key_valid = key_slots[None, :] < lengths_now[:, None]
        queries = rotate(
            split_heads(matmul(token_rows, full_query)), cosine_table, sine_table
        ).astype(jnp.bfloat16)
        keys_local = (
            rotate(split_heads(matmul(token_rows, full_key)), cosine_table, sine_table)
            .astype(jnp.bfloat16)
            .reshape(seq_count, local_len, model_width)
        )
        values_local = (
            matmul(token_rows, full_value)
            .astype(jnp.bfloat16)
            .reshape(seq_count, local_len, model_width)
        )
        keys_all, values_all = (
            lax.all_gather(keys_local, "blk", axis=1, tiled=True),
            lax.all_gather(values_local, "blk", axis=1, tiled=True),
        )
        keys_heads = keys_all.reshape(seq_count, seq_len, head_count, head_dim)
        values_heads = values_all.reshape(seq_count, seq_len, head_count, head_dim)
        summed, log_total = attention_forward(queries, keys_heads, values_heads, key_valid)
        attended = summed.reshape(seq_count * local_len, model_width).astype(jnp.bfloat16)
        residual_one = token_rows.astype(jnp.float32) + matmul(attended, full_output)
        normed, norm_one_back = jax.vjp(
            norm_affine, residual_one, gain_one.astype(jnp.float32), bias_one.astype(jnp.float32)
        )
        normed_low = normed.astype(jnp.bfloat16)
        gate_pre = matmul(normed_low, full_gate)
        up_pre = matmul(normed_low, full_up)
        hidden_full, swiglu_back = jax.vjp(swiglu, gate_pre, up_pre)
        hidden_low = hidden_full.astype(jnp.bfloat16)
        residual_two = normed + matmul(hidden_low, full_down)
        layer_rows, norm_two_back = jax.vjp(
            norm_affine, residual_two, gain_two.astype(jnp.float32), bias_two.astype(jnp.float32)
        )
        layer_list.append(
            jnp.where(row_valid[:, None], layer_rows, 0.0)
            .astype(jnp.bfloat16)
            .reshape(seq_count, local_len, model_width)
        )
        (
            full_query,
            full_key,
            full_value,
            full_output,
            full_gate,
            full_up,
            full_down,
            gain_one,
            bias_one,
            gain_two,
            bias_two,
        ) = (
            lax.all_gather(w_query, "dp", axis=0, tiled=True),
            lax.all_gather(w_key, "dp", axis=0, tiled=True),
            lax.all_gather(w_value, "dp", axis=0, tiled=True),
            lax.all_gather(w_output, "dp", axis=0, tiled=True),
            lax.all_gather(w_gate, "dp", axis=0, tiled=True),
            lax.all_gather(w_up, "dp", axis=0, tiled=True),
            lax.all_gather(w_down, "dp", axis=0, tiled=True),
            lax.all_gather(first_gain, "dp", axis=0, tiled=True),
            lax.all_gather(first_bias, "dp", axis=0, tiled=True),
            lax.all_gather(second_gain, "dp", axis=0, tiled=True),
            lax.all_gather(second_bias, "dp", axis=0, tiled=True),
        )
        keys_all, values_all = (
            lax.all_gather(keys_local, "blk", axis=1, tiled=True),
            lax.all_gather(values_local, "blk", axis=1, tiled=True),
        )
        keys_heads = keys_all.reshape(seq_count, seq_len, head_count, head_dim)
        values_heads = values_all.reshape(seq_count, seq_len, head_count, head_dim)
        upstream = jnp.where(
            row_valid[:, None],
            cotangent[micro_index].reshape(-1, model_width).astype(jnp.float32),
            0.0,
        )
        grad_two, grad_gain_two, grad_bias_two = norm_two_back(upstream)
        grad_ffn = grad_two.astype(jnp.bfloat16)
        grad_down_now = matmul_tn(hidden_low, grad_ffn)
        grad_gate_pre, grad_up_pre = swiglu_back(matmul_nt(grad_ffn, full_down))
        grad_gate_low = grad_gate_pre.astype(jnp.bfloat16)
        grad_up_low = grad_up_pre.astype(jnp.bfloat16)
        grad_gate_now = matmul_tn(normed_low, grad_gate_low)
        grad_up_now = matmul_tn(normed_low, grad_up_low)
        grad_normed = (
            grad_two + matmul_nt(grad_gate_low, full_gate) + matmul_nt(grad_up_low, full_up)
        )
        grad_one, grad_gain_one, grad_bias_one = norm_one_back(grad_normed)
        grad_branch = grad_one.astype(jnp.bfloat16)
        grad_output_now = matmul_tn(attended, grad_branch)
        grad_attended = (
            matmul_nt(grad_branch, full_output)
            .astype(jnp.bfloat16)
            .reshape(seq_count, local_len, head_count, head_dim)
        )
        row_delta = jnp.einsum("snhd,snhd->shn", grad_attended.astype(jnp.float32), summed)
        grad_rotated, key_terms = attention_backward(
            queries, keys_heads, values_heads, key_valid, grad_attended, log_total, row_delta
        )
        key_sums = lax.psum_scatter(
            key_terms.astype(jnp.bfloat16), "blk", scatter_dimension=1, tiled=True
        ).astype(jnp.float32)
        key_part = split_heads(key_sums[..., :model_width])
        value_part = key_sums[..., model_width:]
        grad_queries = (
            unrotate(grad_rotated, cosine_table, sine_table)
            .astype(jnp.bfloat16)
            .reshape(-1, model_width)
        )
        grad_keys = (
            unrotate(key_part, cosine_table, sine_table)
            .astype(jnp.bfloat16)
            .reshape(-1, model_width)
        )
        grad_values = value_part.astype(jnp.bfloat16).reshape(-1, model_width)
        grad_rows = (
            grad_one
            + matmul_nt(grad_queries, full_query)
            + matmul_nt(grad_keys, full_key)
            + matmul_nt(grad_values, full_value)
        )
        grad_list.append(grad_rows.reshape(seq_count, local_len, model_width))
        grad_query_now = matmul_tn(token_rows, grad_queries)
        grad_key_now = matmul_tn(token_rows, grad_keys)
        grad_value_now = matmul_tn(token_rows, grad_values)
        grad_now = (
            lax.psum_scatter(
                grad_query_now.astype(jnp.bfloat16), "dp", scatter_dimension=0, tiled=True
            ).astype(jnp.float32),
            lax.psum_scatter(
                grad_key_now.astype(jnp.bfloat16), "dp", scatter_dimension=0, tiled=True
            ).astype(jnp.float32),
            lax.psum_scatter(
                grad_value_now.astype(jnp.bfloat16), "dp", scatter_dimension=0, tiled=True
            ).astype(jnp.float32),
            lax.psum_scatter(
                grad_output_now.astype(jnp.bfloat16), "dp", scatter_dimension=0, tiled=True
            ).astype(jnp.float32),
            lax.psum_scatter(
                grad_gate_now.astype(jnp.bfloat16), "dp", scatter_dimension=0, tiled=True
            ).astype(jnp.float32),
            lax.psum_scatter(
                grad_up_now.astype(jnp.bfloat16), "dp", scatter_dimension=0, tiled=True
            ).astype(jnp.float32),
            lax.psum_scatter(
                grad_down_now.astype(jnp.bfloat16), "dp", scatter_dimension=0, tiled=True
            ).astype(jnp.float32),
            lax.psum_scatter(
                grad_gain_one.astype(jnp.bfloat16), "dp", scatter_dimension=0, tiled=True
            ).astype(jnp.float32),
            lax.psum_scatter(
                grad_bias_one.astype(jnp.bfloat16), "dp", scatter_dimension=0, tiled=True
            ).astype(jnp.float32),
            lax.psum_scatter(
                grad_gain_two.astype(jnp.bfloat16), "dp", scatter_dimension=0, tiled=True
            ).astype(jnp.float32),
            lax.psum_scatter(
                grad_bias_two.astype(jnp.bfloat16), "dp", scatter_dimension=0, tiled=True
            ).astype(jnp.float32),
        )
        if grad_totals is None:
            grad_totals = tuple(grad_now)
        else:
            grad_totals = tuple(
                (running + addition for running, addition in zip(grad_totals, grad_now))
            )
    cycle_sums = (
        lax.psum(grad_totals[0].astype(jnp.bfloat16), "blk").astype(jnp.float32),
        lax.psum(grad_totals[1].astype(jnp.bfloat16), "blk").astype(jnp.float32),
        lax.psum(grad_totals[2].astype(jnp.bfloat16), "blk").astype(jnp.float32),
        lax.psum(grad_totals[3].astype(jnp.bfloat16), "blk").astype(jnp.float32),
        lax.psum(grad_totals[4].astype(jnp.bfloat16), "blk").astype(jnp.float32),
        lax.psum(grad_totals[5].astype(jnp.bfloat16), "blk").astype(jnp.float32),
        lax.psum(grad_totals[6].astype(jnp.bfloat16), "blk").astype(jnp.float32),
        lax.psum(grad_totals[7].astype(jnp.bfloat16), "blk").astype(jnp.float32),
        lax.psum(grad_totals[8].astype(jnp.bfloat16), "blk").astype(jnp.float32),
        lax.psum(grad_totals[9].astype(jnp.bfloat16), "blk").astype(jnp.float32),
        lax.psum(grad_totals[10].astype(jnp.bfloat16), "blk").astype(jnp.float32),
    )
    layer_out = jnp.stack(layer_list, axis=0)
    grad_tokens = jnp.stack(grad_list, axis=0)
    return (
        layer_out,
        grad_tokens,
        cycle_sums[0],
        cycle_sums[1],
        cycle_sums[2],
        cycle_sums[3],
        cycle_sums[4],
        cycle_sums[5],
        cycle_sums[6],
        cycle_sums[7],
        cycle_sums[8],
        cycle_sums[9],
        cycle_sums[10],
    )


def solution(mesh):
    placed = (
        P(None, "dp", "blk", None),
        P(None, "dp"),
        P("dp", None),
        P("dp", None),
        P("dp", None),
        P("dp", None),
        P("dp", None),
        P("dp", None),
        P("dp", None),
        P("dp"),
        P("dp"),
        P("dp"),
        P("dp"),
        P(None, "dp", "blk", None),
    )
    return jax.shard_map(
        shards,
        mesh=mesh,
        in_specs=placed,
        out_specs=(
            P(None, "dp", "blk", None),
            P(None, "dp", "blk", None),
            P("dp", None),
            P("dp", None),
            P("dp", None),
            P("dp", None),
            P("dp", None),
            P("dp", None),
            P("dp", None),
            P("dp"),
            P("dp"),
            P("dp"),
            P("dp"),
        ),
        check_vma=False,
    )
```

profile of v0, /device:TPU:0, one launch (start us, length us, event | category | flops | bytes accessed | tf_op | source)
XLA Modules:
  0.0 1306.5 jit_solution(9978268645555943159)
XLA Ops:
  9.5 30.9 %all-gather.14.cloned.1.call-done = bf16[768,768]{1,0:T(8,128)(2,1)} async-done(((bf16[192,768]{1,0:T(8,128)(2,1)}), bf16[768,768]{1,0:T(8,128)(2,1)}) %all-gather.14.cloned.1.call-update) | async-done | bytes 1179664 | tf_op jit(solution)/shard_map/all_gather | solution.py:230
  45.3 24.6 %all-gather.18.cloned.1.call-done = bf16[768,768]{1,0:T(8,128)(2,1)} async-done(((bf16[192,768]{1,0:T(8,128)(2,1)}), bf16[768,768]{1,0:T(8,128)(2,1)}) %all-gather.18.cloned.1.call-update) | async-done | bytes 1179664 | tf_op jit(solution)/shard_map/all_gather | solution.py:229
  71.5 28.0 %all-gather.16.cloned.1.call-done = bf16[768,768]{1,0:T(8,128)(2,1)} async-done(((bf16[192,768]{1,0:T(8,128)(2,1)}), bf16[768,768]{1,0:T(8,128)(2,1)}) %all-gather.16.cloned.1.call-update) | async-done | bytes 1179664 | tf_op jit(solution)/shard_map/all_gather | solution.py:228
  112.2 9.0 all-reduce.15
  123.3 3.4 all-gather.34.cloned.1.call-done
  129.3 24.1 %all-gather.32.cloned.1.call-done = bf16[1024,768]{1,0:T(8,128)(2,1)} async-done(((bf16[128,768]{1,0:T(8,128)(2,1)}), bf16[1024,768]{1,0:T(8,128)(2,1)}) %all-gather.32.cloned.1.call-update) | async-done | bytes 1572880 | tf_op jit(solution)/shard_map/all_gather | solution.py:260
  155.1 27.0 %all-gather.30.cloned.1.call-done = bf16[1,1024,768]{1,2,0:T(8,128)(2,1)} async-done(((bf16[1,128,768]{1,2,0:T(8,128)(2,1)}), bf16[1,1024,768]{1,2,0:T(8,128)(2,1)}) %all-gather.30.cloned.1.call-update) | async-done | bytes 1572880 | tf_op jit(solution)/shard_map/all_gather | solution.py:259
  182.1 5.2 fusion.3
  187.3 23.3 %all-gather.20.cloned.1.call-done = bf16[1,1024,768]{1,2,0:T(8,128)(2,1)} async-done(((bf16[1,128,768]{1,2,0:T(8,128)(2,1)}), bf16[1,1024,768]{1,2,0:T(8,128)(2,1)}) %all-gather.20.cloned.1.call-update) | async-done | bytes 1572880 | tf_op jit(solution)/shard_map/all_gather | solution.py:259
  220.4 18.9 %all-gather.22.cloned.1.call-done = bf16[768,768]{1,0:T(8,128)(2,1)} async-done(((bf16[192,768]{1,0:T(8,128)(2,1)}), bf16[768,768]{1,0:T(8,128)(2,1)}) %all-gather.22.cloned.1.call-update) | async-done | bytes 1179664 | tf_op jit(solution)/shard_map/all_gather | solution.py:231
  241.1 5.2 bitcast_convert_fusion.1
  247.4 50.9 %all-gather.24.cloned.1.call-done = bf16[768,3072]{1,0:T(8,128)(2,1)} async-done(((bf16[192,3072]{1,0:T(8,128)(2,1)}), bf16[768,3072]{1,0:T(8,128)(2,1)}) %all-gather.24.cloned.1.call-update) | async-done | bytes 4718608 | tf_op jit(solution)/shard_map/all_gather | solution.py:232
  298.3 4.3 fusion.107
  302.6 54.5 %all-gather.26.cloned.1.call-done = bf16[768,3072]{1,0:T(8,128)(2,1)} async-done(((bf16[192,3072]{1,0:T(8,128)(2,1)}), bf16[768,3072]{1,0:T(8,128)(2,1)}) %all-gather.26.cloned.1.call-update) | async-done | bytes 4718608 | tf_op jit(solution)/shard_map/all_gather | solution.py:233
  357.1 5.0 multiply_convert_fusion.7
  362.1 53.9 %all-gather.28.cloned.1.call-done = bf16[3072,768]{1,0:T(8,128)(2,1)} async-done(((bf16[768,768]{1,0:T(8,128)(2,1)}), bf16[3072,768]{1,0:T(8,128)(2,1)}) %all-gather.28.cloned.1.call-update) | async-done | bytes 4718608 | tf_op jit(solution)/shard_map/all_gather | solution.py:234
  416.1 3.4 fusion.106
  443.5 4.6 convolution_convert_fusion.6
  454.4 15.8 %copy.76 = bf16[1,1024,1536]{2,0,1:T(2,128)(2,1)} copy(bf16[1,1024,1536]{1,2,0:T(8,128)(2,1)} %pad_maximum_fusion.1) | data formatting | bytes 6291456
  470.2 5.2 copy.100
  482.3 5.9 multiply_convert_fusion.1
  494.0 15.8 %copy.74 = bf16[1,1024,1536]{2,0,1:T(2,128)(2,1)} copy(bf16[1,1024,1536]{1,2,0:T(8,128)(2,1)} %pad_maximum_fusion) | data formatting | bytes 6291456
  509.8 5.4 copy.101
  525.0 32.7 %reduce-scatter.49.cloned.1.call-done = bf16[128,1536]{1,0:T(8,128)(2,1)} async-done(((bf16[1024,1536]{1,0:T(8,128)(2,1)}), bf16[128,1536]{1,0:T(8,128)(2,1)}) %reduce-scatter.49.cloned.1.call-update) | async-done | bytes 393232
  565.3 3.4 fusion.20
  580.6 3.6 convolution_convert_fusion
  585.5 3.7 convolution_convert_fusion.1
  590.4 3.6 convolution_convert_fusion.3
  595.2 3.5 convolution_convert_fusion.2
  599.8 3.5 convolution_convert_fusion.5
  604.5 3.6 convolution_convert_fusion.4
  609.6 16.3 %all-reduce.14 = (bf16[768]{0:T(1024)(128)(2,1)S(1)}, bf16[768]{0:T(1024)(128)(2,1)S(1)}, bf16[768]{0:T(1024)(128)(2,1)S(1)}, bf16[768]{0:T(1024)(128)(2,1)S(1)}...) all-reduce(bf16[768]{0:T(1024)(128)(2,1)S(1)} %dynamic-update-slice, ...), channel_id=1, replica_groups=mesh['dp'=4,'blk'=8] {'dp'}, use_global_device_ids=true, to_apply=%add.3 | all-reduce | flops 6912 | bytes 27648
  627.8 23.5 %reduce-scatter.63.cloned.1.call-done = bf16[192,768]{1,0:T(8,128)(2,1)} async-done(((bf16[768,768]{1,0:T(8,128)(2,1)}), bf16[192,768]{1,0:T(8,128)(2,1)}) %reduce-scatter.63.cloned.1.call-update) | async-done | bytes 294928
  652.4 30.2 %reduce-scatter.61.cloned.1.call-done = bf16[192,768]{1,0:T(8,128)(2,1)} async-done(((bf16[768,768]{1,0:T(8,128)(2,1)}), bf16[192,768]{1,0:T(8,128)(2,1)}) %reduce-scatter.61.cloned.1.call-update) | async-done | bytes 294928
  683.8 30.2 %reduce-scatter.57.cloned.1.call-done = bf16[192,768]{1,0:T(8,128)(2,1)} async-done(((bf16[768,768]{1,0:T(8,128)(2,1)}), bf16[192,768]{1,0:T(8,128)(2,1)}) %reduce-scatter.57.cloned.1.call-update) | async-done | bytes 294928
  715.1 30.9 %reduce-scatter.59.cloned.1.call-done = bf16[192,768]{1,0:T(8,128)(2,1)} async-done(((bf16[768,768]{1,0:T(8,128)(2,1)}), bf16[192,768]{1,0:T(8,128)(2,1)}) %reduce-scatter.59.cloned.1.call-update) | async-done | bytes 294928
  747.2 30.8 %reduce-scatter.53.cloned.1.call-done = bf16[192,768]{1,0:T(8,128)(2,1)} async-done(((bf16[768,768]{1,0:T(8,128)(2,1)}), bf16[192,768]{1,0:T(8,128)(2,1)}) %reduce-scatter.53.cloned.1.call-update) | async-done | bytes 294928
  779.1 30.9 %reduce-scatter.55.cloned.1.call-done = bf16[192,768]{1,0:T(8,128)(2,1)} async-done(((bf16[768,768]{1,0:T(8,128)(2,1)}), bf16[192,768]{1,0:T(8,128)(2,1)}) %reduce-scatter.55.cloned.1.call-update) | async-done | bytes 294928
  813.7 56.4 %reduce-scatter.47.cloned.1.call-done = bf16[768,768]{1,0:T(8,128)(2,1)} async-done(((bf16[3072,768]{1,0:T(8,128)(2,1)}), bf16[768,768]{1,0:T(8,128)(2,1)}) %reduce-scatter.47.cloned.1.call-update) | async-done | bytes 1179664 | tf_op jit(solution)/shard_map/reduce_scatter | solution.py:388
  870.1 60.1 %reduce-scatter.45.cloned.1.call-done = bf16[768,768]{1,0:T(8,128)(2,1)} async-done(((bf16[3072,768]{1,0:T(8,128)(2,1)}), bf16[768,768]{1,0:T(8,128)(2,1)}) %reduce-scatter.45.cloned.1.call-update) | async-done | bytes 1179664 | tf_op jit(solution)/shard_map/reduce_scatter | solution.py:388
  933.2 57.1 %reduce-scatter.41.cloned.1.call-done = bf16[192,3072]{1,0:T(8,128)(2,1)} async-done(((bf16[768,3072]{1,0:T(8,128)(2,1)}), bf16[192,3072]{1,0:T(8,128)(2,1)}) %reduce-scatter.41.cloned.1.call-update) | async-done | bytes 1179664 | tf_op jit(solution)/shard_map/reduce_scatter | solution.py:385
  990.2 60.1 %reduce-scatter.43.cloned.1.call-done = bf16[192,3072]{1,0:T(8,128)(2,1)} async-done(((bf16[768,3072]{1,0:T(8,128)(2,1)}), bf16[192,3072]{1,0:T(8,128)(2,1)}) %reduce-scatter.43.cloned.1.call-update) | async-done | bytes 1179664 | tf_op jit(solution)/shard_map/reduce_scatter | solution.py:385
  1050.4 3.0 add_convert_fusion.1
  1053.4 56.9 %reduce-scatter.37.cloned.1.call-done = bf16[192,3072]{1,0:T(8,128)(2,1)} async-done(((bf16[768,3072]{1,0:T(8,128)(2,1)}), bf16[192,3072]{1,0:T(8,128)(2,1)}) %reduce-scatter.37.cloned.1.call-update) | async-done | bytes 1179664 | tf_op jit(solution)/shard_map/reduce_scatter | solution.py:382
  1110.3 60.0 %reduce-scatter.39.cloned.1.call-done = bf16[192,3072]{1,0:T(8,128)(2,1)} async-done(((bf16[768,3072]{1,0:T(8,128)(2,1)}), bf16[192,3072]{1,0:T(8,128)(2,1)}) %reduce-scatter.39.cloned.1.call-update) | async-done | bytes 1179664 | tf_op jit(solution)/shard_map/reduce_scatter | solution.py:382
  1170.3 3.0 add_convert_fusion.2
  1173.7 16.8 %all-reduce.12 = (bf16[192]{0:T(256)(128)(2,1)S(1)}, bf16[192]{0:T(256)(128)(2,1)S(1)}, bf16[192]{0:T(256)(128)(2,1)S(1)}, bf16[192]{0:T(256)(128)(2,1)S(1)}) all-reduce(bf16[192]{0:T(256)(128)(2,1)S(1)} %add_convert_fusion.18, bf16[192]{0:T(256)(128)(2,1)S(1)} %add_convert_fusion.17, ...), channel_id=1, replica_groups=mesh['dp'=4,'blk'=8] {'blk'}, use_global_device_ids=true, to_apply=%region_47.48 | all-reduce | flops 768 | bytes 3072 | tf_op jit(solution)/shard_map/psum | solution.py:418
  1199.3 89.9 %all-reduce.18.cloned.1.call-done = (bf16[192,768]{0,1:T(8,128)(2,1)}, bf16[192,768]{0,1:T(8,128)(2,1)}, bf16[192,768]{0,1:T(8,128)(2,1)}, bf16[192,768]{1,0:T(8...) async-done(((bf16[192,768]{0,1:T(8,128)(2,1)}, bf16[192,768]{0,1:T(8,128)(2,1)}, bf16[192,768]{0,1:T(8,128)(2,1)}, ...) | async-done | bytes 4718608 | tf_op jit(solution)/shard_map/psum | solution.py:411
  (448 shorter events, 150.2 us)
Async XLA Ops:
  7.2 35.6 %copy-start.3 = (bf16[2,1,128,768]{3,2,1,0:T(8,128)(2,1)S(1)}, bf16[2,1,128,768]{3,2,1,0:T(8,128)(2,1)}, u32[]{:S(2)}) copy-start(bf16[2,1,128,768]{3,2,1,0:T(8,128)(2,1)} %param.14) | copy-start | bytes 1179652
  7.2 33.1 %all-gather.14.cloned.1.call-start = ((), (), s32[]{:S(2)}) async-start(), calls=%async_computation.16 | async-start | bytes 1474560 | tf_op jit(solution)/shard_map/all_gather | solution.py:230
  7.9 62.0 %all-gather.18.cloned.1.call-start = ((), (), s32[]{:S(2)}) async-start(), calls=%async_computation.18 | async-start | bytes 1474560 | tf_op jit(solution)/shard_map/all_gather | solution.py:229
  8.7 90.8 %all-gather.16.cloned.1.call-start = ((), (), s32[]{:S(2)}) async-start(), calls=%async_computation.17 | async-start | bytes 1474560 | tf_op jit(solution)/shard_map/all_gather | solution.py:228
  9.4 117.3 %all-gather.34.cloned.1.call-start = ((), (), s32[]{:S(2)}) async-start(), calls=%async_computation.34 | async-start | bytes 1769472 | tf_op jit(solution)/shard_map/all_gather | solution.py:260
  42.7 110.6 %all-gather.32.cloned.1.call-start = ((), (), s32[]{:S(2)}) async-start(), calls=%async_computation.33 | async-start | bytes 1769472 | tf_op jit(solution)/shard_map/all_gather | solution.py:260
  45.1 137.0 %all-gather.30.cloned.1.call-start = ((), (), s32[]{:S(2)}) async-start(), calls=%async_computation.24 | async-start | bytes 1769472 | tf_op jit(solution)/shard_map/all_gather | solution.py:259
  104.4 77.8 %copy-start.62 = (bf16[128,12,32]{0,2,1:T(8,128)(2,1)}, bf16[128,12,32]{0,2,1:T(8,128)(2,1)S(1)}, u32[]{:S(2)}) copy-start(bf16[128,12,32]{0,2,1:T(8,128)(2,1)S(1)} %get-tuple-element.287) | copy-start | bytes 294916
  104.4 77.7 %copy-start.64 = (bf16[128,12,32]{0,2,1:T(8,128)(2,1)}, bf16[128,12,32]{0,2,1:T(8,128)(2,1)S(1)}, u32[]{:S(2)}) copy-start(bf16[128,12,32]{0,2,1:T(8,128)(2,1)S(1)} %get-tuple-element.288) | copy-start | bytes 294916
  104.4 106.2 %copy-start.58 = (bf16[128,12,32]{0,2,1:T(8,128)(2,1)}, bf16[128,12,32]{0,2,1:T(8,128)(2,1)S(1)}, u32[]{:S(2)}) copy-start(bf16[128,12,32]{0,2,1:T(8,128)(2,1)S(1)} %get-tuple-element.269) | copy-start | bytes 294916
  104.4 106.2 %copy-start.60 = (bf16[128,12,32]{0,2,1:T(8,128)(2,1)}, bf16[128,12,32]{0,2,1:T(8,128)(2,1)S(1)}, u32[]{:S(2)}) copy-start(bf16[128,12,32]{0,2,1:T(8,128)(2,1)S(1)} %get-tuple-element.270) | copy-start | bytes 294916
  105.2 105.4 %all-gather.20.cloned.1.call-start = ((), (), s32[]{:S(2)}) async-start(), calls=%async_computation.19 | async-start | bytes 1769472 | tf_op jit(solution)/shard_map/all_gather | solution.py:259
  106.0 133.4 %all-gather.22.cloned.1.call-start = ((), (), s32[]{:S(2)}) async-start(), calls=%async_computation.20 | async-start | bytes 1474560 | tf_op jit(solution)/shard_map/all_gather | solution.py:231
  106.8 191.6 %all-gather.24.cloned.1.call-start = ((), (), s32[]{:S(2)}) async-start(), calls=%async_computation.21 | async-start | bytes 5898240 | tf_op jit(solution)/shard_map/all_gather | solution.py:232
  107.5 249.6 %all-gather.26.cloned.1.call-start = ((), (), s32[]{:S(2)}) async-start(), calls=%async_computation.22 | async-start | bytes 5898240 | tf_op jit(solution)/shard_map/all_gather | solution.py:233
  108.1 308.0 %all-gather.28.cloned.1.call-start = ((), (), s32[]{:S(2)}) async-start(), calls=%async_computation.23 | async-start | bytes 5898240 | tf_op jit(solution)/shard_map/all_gather | solution.py:234
  108.8 410.8 %reduce-scatter.51.cloned.1.call-start = ((), (), s32[]{:S(2)}) async-start(), calls=%async_computation.36 | async-start | bytes 3538944
  110.1 107.6 %copy-start.95 = (pred[1024]{0:T(1024)(128)(4,1)}, pred[1024]{0:T(1024)(128)(4,1)S(1)}, u32[]{:S(2)}) copy-start(pred[1024]{0:T(1024)(128)(4,1)S(1)} %iota_compare_fusion) | copy-start | bytes 3076
  122.0 119.1 %copy-start.97 = (pred[1024]{0:T(1024)(128)(4,1)}, pred[1024]{0:T(1024)(128)(4,1)S(1)}, u32[]{:S(2)}) copy-start(pred[1024]{0:T(1024)(128)(4,1)S(1)} %iota_compare_fusion.1) | copy-start | bytes 3076
  155.1 86.0 %copy-start.49 = (bf16[1024,768]{0,1:T(8,128)(2,1)}, bf16[1024,768]{0,1:T(8,128)(2,1)S(1)}, u32[]{:S(2)}) copy-start(bf16[1024,768]{0,1:T(8,128)(2,1)S(1)} %copy.49) | copy-start | bytes 4718596
  217.7 23.4 %copy-start.81 = (f32[12,128]{1,0:T(8,128)}, f32[12,128]{1,0:T(8,128)S(1)}, u32[]{:S(2)}) copy-start(f32[12,128]{1,0:T(8,128)S(1)} %log_add_fusion.1) | copy-start | bytes 18436
  220.4 25.9 %copy-start.70 = (bf16[1,128,12,64]{1,3,2,0:T(8,128)(2,1)}, bf16[1,128,12,64]{1,3,2,0:T(8,128)(2,1)S(1)}, u32[]{:S(2)}) copy-start(bf16[1,128,12,64]{1,3,2,0:T(8,128)(2,1)S(1)} %get-tuple-element.314) | copy-start | bytes 589828
  247.4 109.7 %copy-start.20 = (bf16[128,768]{1,0:T(8,128)(2,1)}, bf16[128,768]{1,0:T(8,128)(2,1)S(1)}, u32[]{:S(2)}) copy-start(bf16[128,768]{1,0:T(8,128)(2,1)S(1)} %get-tuple-element.293) | copy-start | bytes 589828
  362.1 57.3 %copy-start.22 = (bf16[128,3072]{1,0:T(8,128)(2,1)}, bf16[128,3072]{1,0:T(8,128)(2,1)S(1)}, u32[]{:S(2)}) copy-start(bf16[128,3072]{1,0:T(8,128)(2,1)S(1)} %get-tuple-element.318) | copy-start | bytes 2359300
  475.5 82.3 %reduce-scatter.49.cloned.1.call-start = ((), (), s32[]{:S(2)}) async-start(), calls=%async_computation.35 | async-start | bytes 3538944
  476.6 13.4 %slice-start = ((s8[6291456]{0:T(1024)(128)(4,1)}), s8[2097152]{0:T(1024)(128)(4,1)S(1)}, s32[]{:S(2)}) async-start(s8[6291456]{0:T(1024)(128)(4,1)} %bitcast.272), calls=%async_computation.44 | async-start | bytes 4194304
  482.3 7.7 slice-start.1
  515.3 110.6 %reduce-scatter.35.cloned.1.call-start = ((), (), s32[]{:S(2)}) async-start(), calls=%async_computation.26 | async-start | bytes 1474560 | tf_op jit(solution)/shard_map/reduce_scatter | solution.py:379
  517.9 108.0 %reduce-scatter.33.cloned.1.call-start = ((), (), s32[]{:S(2)}) async-start(), calls=%async_computation.25 | async-start | bytes 1474560 | tf_op jit(solution)/shard_map/reduce_scatter | solution.py:379
  519.6 131.7 %reduce-scatter.63.cloned.1.call-start = ((), (), s32[]{:S(2)}) async-start(), calls=%async_computation.42 | async-start | bytes 1474560
  525.0 157.7 %reduce-scatter.61.cloned.1.call-start = ((), (), s32[]{:S(2)}) async-start(), calls=%async_computation.41 | async-start | bytes 1474560
  565.0 149.0 %reduce-scatter.57.cloned.1.call-start = ((), (), s32[]{:S(2)}) async-start(), calls=%async_computation.39 | async-start | bytes 1474560
  573.7 172.3 %reduce-scatter.59.cloned.1.call-start = ((), (), s32[]{:S(2)}) async-start(), calls=%async_computation.40 | async-start | bytes 1474560
  575.8 202.1 %reduce-scatter.53.cloned.1.call-start = ((), (), s32[]{:S(2)}) async-start(), calls=%async_computation.37 | async-start | bytes 1474560
  577.8 232.2 %reduce-scatter.55.cloned.1.call-start = ((), (), s32[]{:S(2)}) async-start(), calls=%async_computation.38 | async-start | bytes 1474560
  580.5 289.6 %reduce-scatter.47.cloned.1.call-start = ((), (), s32[]{:S(2)}) async-start(), calls=%async_computation.32 | async-start | bytes 5898240 | tf_op jit(solution)/shard_map/reduce_scatter | solution.py:388
  584.3 346.0 %reduce-scatter.45.cloned.1.call-start = ((), (), s32[]{:S(2)}) async-start(), calls=%async_computation.31 | async-start | bytes 5898240 | tf_op jit(solution)/shard_map/reduce_scatter | solution.py:388
  589.2 401.0 %reduce-scatter.41.cloned.1.call-start = ((), (), s32[]{:S(2)}) async-start(), calls=%async_computation.29 | async-start | bytes 5898240 | tf_op jit(solution)/shard_map/reduce_scatter | solution.py:385
  594.1 456.3 %reduce-scatter.43.cloned.1.call-start = ((), (), s32[]{:S(2)}) async-start(), calls=%async_computation.30 | async-start | bytes 5898240 | tf_op jit(solution)/shard_map/reduce_scatter | solution.py:385
  598.7 511.6 %reduce-scatter.37.cloned.1.call-start = ((), (), s32[]{:S(2)}) async-start(), calls=%async_computation.27 | async-start | bytes 5898240 | tf_op jit(solution)/shard_map/reduce_scatter | solution.py:382
  603.4 566.9 %reduce-scatter.39.cloned.1.call-start = ((), (), s32[]{:S(2)}) async-start(), calls=%async_computation.28 | async-start | bytes 5898240 | tf_op jit(solution)/shard_map/reduce_scatter | solution.py:382
  608.1 681.1 %all-reduce.18.cloned.1.call-start = ((), (), s32[]{:S(2)}) async-start(), calls=%async_computation.43 | async-start | bytes 10027008 | tf_op jit(solution)/shard_map/psum | solution.py:411
  1173.3 19.4 %copy-start.86 = (f32[128]{0:T(128)S(1)}, f32[128]{0:T(128)}, u32[]{:S(2)}) copy-start(f32[128]{0:T(128)} %copy-done.85) | copy-start | bytes 1540
  1173.3 19.4 %copy-start.88 = (f32[128]{0:T(128)S(1)}, f32[128]{0:T(128)}, u32[]{:S(2)}) copy-start(f32[128]{0:T(128)} %copy-done.87) | copy-start | bytes 1540
  1173.3 20.5 %copy-start.12 = (bf16[768,768]{1,0:T(8,128)(2,1)S(1)}, bf16[768,768]{1,0:T(8,128)(2,1)}, u32[]{:S(2)}) copy-start(bf16[768,768]{1,0:T(8,128)(2,1)} %all-gather.16.cloned.1.call-done) | copy-start | bytes 3538948
  1173.4 20.5 %copy-start.94 = (f32[128]{0:T(128)S(1)}, f32[128]{0:T(128)}, u32[]{:S(2)}) copy-start(f32[128]{0:T(128)} %copy-done.92) | copy-start | bytes 1540
  1173.4 22.2 %copy-start.11 = (bf16[768,768]{1,0:T(8,128)(2,1)S(1)}, bf16[768,768]{1,0:T(8,128)(2,1)}, u32[]{:S(2)}) copy-start(bf16[768,768]{1,0:T(8,128)(2,1)} %all-gather.18.cloned.1.call-done) | copy-start | bytes 3538948
  1173.4 22.2 %copy-start.39 = (bf16[1,128,12,64]{1,3,2,0:T(8,128)(2,1)S(1)}, bf16[1,128,12,64]{1,3,2,0:T(8,128)(2,1)}, u32[]{:S(2)}) copy-start(bf16[1,128,12,64]{1,3,2,0:T(8,128)(2,1)} %copy-done.38) | copy-start | bytes 589828
  (97 other events, 257.1 us)
Sparse Core Ops, SparseCore 0:
  9.9 30.4 all-gather.13
  42.2 27.7 all-gather.17
  71.8 27.7 all-gather.15
  101.6 25.0 all-gather.33
  128.7 24.5 all-gather.31
  155.4 26.6 all-gather.29
  184.3 26.3 all-gather.19
  212.5 26.8 all-gather.21
  241.2 57.0 all-gather.23
  300.0 57.0 all-gather.25
  359.0 57.0 all-gather.27
  475.6 40.3 reduce-scatter.50
  518.3 39.4 reduce-scatter.48
  560.5 27.6 reduce-scatter.34
  590.9 28.8 reduce-scatter.32
  622.6 28.6 reduce-scatter.62
  654.1 28.5 reduce-scatter.60
  685.4 28.5 reduce-scatter.56
  717.5 28.5 reduce-scatter.58
  749.4 28.5 reduce-scatter.52
  781.4 28.5 reduce-scatter.54
  813.0 57.0 reduce-scatter.46
  873.1 57.0 reduce-scatter.44
  933.1 57.0 reduce-scatter.40
  993.2 57.0 reduce-scatter.42
  1053.2 57.0 reduce-scatter.36
  1113.2 57.0 reduce-scatter.38
  1174.4 114.7 all-reduce.17
where the time goes:
time: 1320 us; the launch traced here: 1310 us
  waiting for transfers between devices  994 us (75%)
  matrix products  109 us (8%)
  local copies, waits for them, and re-layouts  98.7 us (7%)
  other arithmetic  42.7 us (3%)
  blocking collectives  42.1 us (3%)
  between operations  18 us (1%)
    unnamed x36, waiting for transfers between devices  214 us
    reduce_scatter x2, waiting for transfers between devices, shards(): lax.psum_scatter(grad_up_now.astype(jnp.bfloat16), 'dp', scatter_dimensio...  117 us
    reduce_scatter x2, waiting for transfers between devices, shards(): lax.psum_scatter(grad_gate_now.astype(jnp.bfloat16), 'dp', scatter_dimens...  117 us
    reduce_scatter x2, waiting for transfers between devices, shards(): lax.psum_scatter(grad_down_now.astype(jnp.bfloat16), 'dp', scatter_dimens...  117 us
    psum x1, waiting for transfers between devices, shards(): lax.psum(grad_totals[0].astype(jnp.bfloat16), 'blk').astype(jnp.float32)  89.9 us
    unnamed x268, local copies, waits for them, and re-layouts  83.3 us
    all_gather x1, waiting for transfers between devices, shards(): lax.all_gather(w_up, 'dp', axis=0, tiled=True)  54.5 us
    all_gather x1, waiting for transfers between devices, shards(): lax.all_gather(w_down, 'dp', axis=0, tiled=True)  53.9 us
  transfers between devices with their start and end apart: 28, of which 25 were waited for; matrix products, arithmetic and copies ran while one was open for 13% of the time, Pallas kernels for 0%

commit v1 on v0

v1 whole, which is shorter than its diff:
```python
import functools

import jax
import jax.numpy as jnp
import numpy as np
from jax import lax
from jax.experimental import pallas as pl
from jax.experimental.pallas import tpu as pltpu
from jax.sharding import PartitionSpec as P

HEAD_DIM = 64
WIDE = 128
PARTS = 4
LOW, FULL = jnp.bfloat16, jnp.float32
VMEM_BYTES = 60 * 1024 * 1024


def mm(left, right):
    return jnp.dot(left, right, preferred_element_type=FULL)


def mm_nt(left, right):
    return lax.dot_general(left, right, (((1,), (1,)), ((), ())), preferred_element_type=FULL)


def mm_tn(left, right):
    return lax.dot_general(left, right, (((0,), (0,)), ((), ())), preferred_element_type=FULL)


def hop(value, axis, bit):
    size = lax.axis_size(axis)
    return lax.ppermute(value, axis, [(at, at ^ bit) for at in range(size)])


def position_table(seq_len):
    half = HEAD_DIM // 2
    frequency = np.float32(1000.0) ** (-(np.arange(half, dtype=np.float32) * np.float32(2.0) / np.float32(HEAD_DIM)))
    angles = np.arange(seq_len, dtype=np.float32)[:, None] * frequency[None, :]
    cosine = np.cos(angles).astype(np.float32)
    sine = np.sin(angles).astype(np.float32)
    place = np.broadcast_to(np.arange(seq_len, dtype=np.float32)[:, None], (seq_len, WIDE))
    return np.concatenate([cosine] * 4 + [sine, sine, -sine, -sine, place], axis=1)


def swap_matrix(heads):
    half = HEAD_DIM // 2
    out = np.zeros((heads * HEAD_DIM, heads * WIDE), np.float32)
    for h in range(heads):
        for f in range(HEAD_DIM):
            out[h * HEAD_DIM + f, h * WIDE + f] = 1.0
        for f in range(half):
            out[h * HEAD_DIM + half + f, h * WIDE + HEAD_DIM + f] = -1.0
            out[h * HEAD_DIM + f, h * WIDE + HEAD_DIM + half + f] = 1.0
    return out


def spread_matrix(heads):
    out = np.zeros((heads * HEAD_DIM, heads * WIDE), np.float32)
    for h in range(heads):
        for f in range(HEAD_DIM):
            out[h * HEAD_DIM + f, h * WIDE + f] = 1.0
    return out


def project_kernel(heads, block, x_ref, w_ref, swap_ref, spread_ref, table_ref, q_ref, k_ref, v_ref):
    parts = w_ref.shape[0]

    def weight(which, matrix):
        rows = jnp.concatenate([w_ref[d, which] for d in range(parts)], axis=0)
        return mm(rows, matrix).astype(LOW)

    w_q = weight(0, swap_ref[...])
    w_k = weight(1, swap_ref[...])
    w_v = weight(2, spread_ref[...])
    for start in range(0, x_ref.shape[0], block):
        rows = slice(start, start + block)
        x = x_ref[rows, :]
        cosine, sine = table_ref[rows, :WIDE], table_ref[rows, WIDE : 2 * WIDE]
        for out_ref, w, scale in ((q_ref, w_q, 0.0625), (k_ref, w_k, None)):
            made = mm(x, w)
            for h in range(heads):
                one = made[:, h * WIDE : (h + 1) * WIDE]
                turned = (one * cosine + pltpu.roll(one, HEAD_DIM, 1) * sine).astype(LOW)
                if scale is not None:
                    turned = turned * jnp.asarray(scale, LOW)
                out_ref[h, rows, :] = turned
        made = mm(x, w_v).astype(LOW)
        for h in range(heads):
            v_ref[h, rows, :] = made[:, h * WIDE : (h + 1) * WIDE]


def attend_kernel(heads, block, len_ref, q_ref, k_ref, v_ref, table_ref, spread_ref, out_ref, lse_ref, bias_ref, wide_ref):
    row_count = q_ref.shape[1]
    place = table_ref[:, 2 * WIDE :]
    bias_ref[...] = jnp.where(place < len_ref[0, 0], 0.0, -1e30)
    for h in range(heads):
        keys = k_ref[h]
        values_t = v_ref[h].T

        def step(number, carry, h=h, keys=keys, values_t=values_t):
            rows = pl.ds(pl.multiple_of(number * block, block), block)
            bias = jnp.concatenate([bias_ref[...]] * (block // WIDE), axis=1)
            scores = mm_nt(keys, q_ref[h, rows, :]) + bias
            top = jnp.max(scores, axis=0, keepdims=True)
            weights = jnp.exp(scores - top)
            total = jnp.sum(weights, axis=0, keepdims=True)
            lse_ref[h, :, rows] = top + jnp.log(total)
            summed = mm(values_t, weights.astype(LOW)) / total
            wide_ref[rows, h * WIDE : (h + 1) * WIDE] = summed.T.astype(LOW)
            return carry

        lax.fori_loop(0, row_count // block, step, 0)
    out_ref[...] = mm_nt(wide_ref[...], spread_ref[...]).astype(LOW)


def attend_back_kernel(
    heads, block, len_ref, q_ref, k_ref, v_ref, table_ref, spread_ref, lse_ref, grad_ref,
    dq_ref, dk_ref, dv_ref, bias_ref, grad_wide_ref, dq_wide_ref, dk_wide_ref, dv_wide_ref, dk_sum_ref, dv_sum_ref,
):
    row_count = q_ref.shape[1]
    place = table_ref[:, 2 * WIDE :]
    bias_ref[...] = jnp.where(place < len_ref[0, 0], 0.0, -1e30)
    grad_wide_ref[...] = mm(grad_ref[...], spread_ref[...]).astype(LOW)

    def unturn(value, rows):
        cosine, sine = table_ref[rows, :WIDE], table_ref[rows, WIDE : 2 * WIDE]
        return (value * cosine - pltpu.roll(value, HEAD_DIM, 1) * sine).astype(LOW)

    for h in range(heads):
        lanes = slice(h * WIDE, (h + 1) * WIDE)
        keys, values = k_ref[h], v_ref[h]
        keys_t = keys.T
        dk_sum_ref[...] = jnp.zeros_like(dk_sum_ref)
        dv_sum_ref[...] = jnp.zeros_like(dv_sum_ref)

        def step(number, carry, h=h, lanes=lanes, keys=keys, values=values, keys_t=keys_t):
            rows = pl.ds(pl.multiple_of(number * block, block), block)
            bias = jnp.concatenate([bias_ref[...]] * (block // WIDE), axis=1)
            queries, grads = q_ref[h, rows, :], grad_wide_ref[rows, lanes]
            probs = jnp.exp(mm_nt(keys, queries) + bias - lse_ref[h, :, rows])
            grad_probs = mm_nt(values, grads)
            delta = jnp.sum(probs * grad_probs, axis=0, keepdims=True)
            grad_scores = (probs * (grad_probs - delta)).astype(LOW)
            dv_sum_ref[...] += mm(probs.astype(LOW), grads)
            dk_sum_ref[...] += mm(grad_scores, queries)
            dq = mm(keys_t, grad_scores).T * 0.125
            dq_wide_ref[rows, lanes] = unturn(dq, rows)
            return carry

        lax.fori_loop(0, row_count // block, step, 0)
        dk_wide_ref[:, lanes] = unturn(dk_sum_ref[...] * 2.0, slice(None))
        dv_wide_ref[:, lanes] = dv_sum_ref[...].astype(LOW)
    for out_ref, wide_ref in ((dq_ref, dq_wide_ref), (dk_ref, dk_wide_ref), (dv_ref, dv_wide_ref)):
        out_ref[...] = mm_nt(wide_ref[...], spread_ref[...]).astype(LOW)


VMEM = pl.BlockSpec(memory_space=pltpu.VMEM)
SMEM = pl.BlockSpec(memory_space=pltpu.SMEM)


def kernel_call(body, outs, in_specs, scratch, flops, exps, *operands):
    moved = sum(o.size * o.dtype.itemsize for o in (*operands, *outs))
    return pl.pallas_call(
        body,
        out_shape=outs,
        in_specs=in_specs,
        out_specs=[VMEM] * len(outs),
        scratch_shapes=scratch,
        compiler_params=pltpu.CompilerParams(vmem_limit_bytes=VMEM_BYTES),
        cost_estimate=pl.CostEstimate(flops=flops, bytes_accessed=moved, transcendentals=exps),
    )(*operands)


def project(x, w, swap, spread, table, heads):
    rows, width = x.shape
    shape = jax.ShapeDtypeStruct((heads, rows, WIDE), LOW)
    return kernel_call(
        functools.partial(project_kernel, heads, min(256, rows)), [shape] * 3, [VMEM] * 5, [],
        2 * rows * width * 3 * heads * WIDE, 0, x, w, swap, spread, table,
    )


def attend(length, q, k, v, table, spread):
    heads, rows, _ = q.shape
    keys = k.shape[1]
    outs = [
        jax.ShapeDtypeStruct((rows, heads * HEAD_DIM), LOW),
        jax.ShapeDtypeStruct((heads, 1, rows), FULL),
    ]
    scratch = [pltpu.VMEM((keys, WIDE), FULL), pltpu.VMEM((rows, heads * WIDE), LOW)]
    return kernel_call(
        functools.partial(attend_kernel, heads, min(256, rows)), outs, [SMEM] + [VMEM] * 5, scratch,
        4 * heads * rows * keys * WIDE, heads * rows * keys, length, q, k, v, table, spread,
    )


def attend_back(length, q, k, v, table, spread, lse, grad):
    heads, rows, _ = q.shape
    keys = k.shape[1]
    outs = [jax.ShapeDtypeStruct((count, heads * HEAD_DIM), LOW) for count in (rows, keys, keys)]
    scratch = [
        pltpu.VMEM((keys, WIDE), FULL),
        pltpu.VMEM((rows, heads * WIDE), LOW),
        pltpu.VMEM((rows, heads * WIDE), LOW),
        pltpu.VMEM((keys, heads * WIDE), LOW),
        pltpu.VMEM((keys, heads * WIDE), LOW),
        pltpu.VMEM((keys, WIDE), FULL),
        pltpu.VMEM((keys, WIDE), FULL),
    ]
    return kernel_call(
        functools.partial(attend_back_kernel, heads, min(256, rows)), outs, [SMEM] + [VMEM] * 7, scratch,
        10 * heads * rows * keys * WIDE, heads * rows * keys, length, q, k, v, table, spread, lse, grad,
    )


def gather_rows(piece, place):
    count = lax.axis_size("dp")
    if count != 4:
        return lax.all_gather(piece, "dp", axis=0, tiled=False)
    axis = piece.ndim - 2
    half = piece.shape[axis] // 2
    from_x, from_y = hop(piece, "dp", 1), hop(piece, "dp", 2)
    far_a = hop(lax.slice_in_dim(from_x, 0, half, axis=axis), "dp", 2)
    far_b = hop(lax.slice_in_dim(from_y, half, 2 * half, axis=axis), "dp", 1)
    far = jnp.concatenate([far_a, far_b], axis=axis)
    out = jnp.zeros((count,) + piece.shape, piece.dtype)
    for distance, part in enumerate((piece, from_x, from_y, far)):
        out = lax.dynamic_update_index_in_dim(out, part, place ^ distance, 0)
    return out


def scatter_rows(terms, place):
    count = lax.axis_size("dp")
    if count != 4:
        return lax.psum_scatter(terms, "dp", scatter_dimension=0, tiled=False).astype(FULL)
    half = terms.shape[1] // 2
    own, near_x, near_y, far = (
        lax.dynamic_index_in_dim(terms, place ^ distance, 0, keepdims=False) for distance in range(4)
    )
    got_x = hop(jnp.concatenate([near_x[:half], far[:half]]), "dp", 1).astype(FULL)
    got_y = hop(jnp.concatenate([near_y[half:], far[half:]]), "dp", 2).astype(FULL)
    low_sum, low_next = own[:half] + got_x[:half], near_y[:half] + got_x[half:]
    high_sum, high_next = own[half:] + got_y[:half], near_x[half:] + got_y[half:]
    low_sum = low_sum + hop(low_next.astype(LOW), "dp", 2).astype(FULL)
    high_sum = high_sum + hop(high_next.astype(LOW), "dp", 1).astype(FULL)
    return jnp.concatenate([low_sum, high_sum])


def bits_between(low, high):
    bits = []
    while low < high:
        bits.append(low)
        low *= 2
    return bits


def sum_bits(value, place, bits):
    for bit in bits:
        half = value.shape[0] // 2
        upper = (place // bit) % 2
        keep = lax.dynamic_slice_in_dim(value, upper * half, half, 0)
        send = lax.dynamic_slice_in_dim(value, (1 - upper) * half, half, 0)
        value = keep + hop(send.astype(LOW), "blk", bit).astype(FULL)
    value = value.astype(LOW)
    for bit in reversed(bits):
        other = hop(value, "blk", bit)
        upper = (place // bit) % 2 == 1
        value = jnp.where(upper, jnp.concatenate([other, value]), jnp.concatenate([value, other]))
    return value


def fold_rows(part):
    half = part.shape[0] // 2
    return part[:half] + hop(part[half:].astype(LOW), "blk", 1).astype(FULL)


def both_rows(own):
    return jnp.concatenate([own, hop(own, "blk", 1)])


def norm_parts(rows):
    centred = rows - jnp.mean(rows, axis=-1, keepdims=True)
    scale = lax.rsqrt(jnp.mean(centred * centred, axis=-1, keepdims=True) + 1e-05)
    return centred * scale, scale


def norm_back(upstream, gain, unit, scale):
    inner = upstream * gain
    grad = (
        inner
        - jnp.mean(inner, axis=-1, keepdims=True)
        - unit * jnp.mean(inner * unit, axis=-1, keepdims=True)
    ) * scale
    return grad, jnp.sum(upstream * unit, axis=0), jnp.sum(upstream, axis=0)


def shards(
    tokens, lengths, w_query, w_key, w_value, w_output, w_gate, w_up, w_down,
    first_gain, first_bias, second_gain, second_bias, cotangent,
):
    _, _, local, width = tokens.shape
    dp_count, blk_count = lax.axis_size("dp"), lax.axis_size("blk")
    dp, blk = lax.axis_index("dp"), lax.axis_index("blk")
    side = blk_count // 2
    which = blk // side
    first = which == 0
    core = blk % 2
    part = blk % PARTS
    heads = width // HEAD_DIM // PARTS
    columns = heads * HEAD_DIM
    spread_bits = bits_between(PARTS, side)
    table = jnp.asarray(position_table(local * blk_count))
    swap = jnp.asarray(swap_matrix(heads), LOW)
    spread = jnp.asarray(spread_matrix(heads), LOW)

    def mine(source):
        return jnp.where(first, source[0, 0], source[1, 0])

    def theirs(source):
        return jnp.where(first, source[1, 0], source[0, 0])

    own_half = mine(tokens)
    got_half = hop(theirs(tokens), "blk", side)
    x_own = jnp.concatenate([own_half, got_half])
    x_core = hop(x_own, "blk", 1)
    x_near = hop(x_own, "blk", 2)
    x_far = hop(x_near, "blk", 1)
    x_all = jnp.concatenate([x_own, x_core, x_near, x_far])

    rows = w_query.shape[0]
    w_qkv = jnp.stack(
        [lax.dynamic_slice_in_dim(w, part * columns, columns, 1) for w in (w_query, w_key, w_value)]
    )
    all_qkv = gather_rows(w_qkv, dp)
    half_width = width // 2
    vectors = jnp.stack([first_gain, first_bias, second_gain, second_bias]).reshape(-1)
    extra_rows = -(-vectors.shape[0] // half_width)

    def pad_extra(flat):
        lead = flat.shape[:-1]
        flat = jnp.pad(flat, [(0, 0)] * len(lead) + [(0, 32 * half_width - flat.shape[-1])])
        return flat.reshape(*lead, 32, half_width)

    w_out_half = lax.dynamic_slice_in_dim(w_output, core * half_width, half_width, 1)
    all_out = gather_rows(jnp.concatenate([w_out_half, pad_extra(vectors)]), dp)
    all_vectors = all_out[:, rows : rows + extra_rows].reshape(dp_count, -1)[:, : vectors.shape[0]]
    all_vectors = all_vectors.reshape(dp_count, 4, rows).transpose(1, 0, 2).reshape(4, width).astype(FULL)
    gain_one, bias_one, gain_two, bias_two = all_vectors

    ff_rows = w_down.shape[0]
    ff_half = ff_rows // 2

    def core_columns(w):
        w = w.reshape(rows, dp_count, 2, ff_half)
        return jnp.where(core == 0, w[:, :, 0], w[:, :, 1]).reshape(rows, dp_count * ff_half)

    full_gate = gather_rows(core_columns(w_gate), dp).reshape(width, dp_count * ff_half)
    full_up = gather_rows(core_columns(w_up), dp).reshape(width, dp_count * ff_half)
    down_half = lax.dynamic_slice_in_dim(w_down, core * ff_half, ff_half, 0)
    full_down = gather_rows(down_half, dp).reshape(dp_count * ff_half, width)

    out_rows = all_out[:, :rows].reshape(PARTS, columns, half_width)

    def head_rows(distance):
        return lax.dynamic_index_in_dim(out_rows, part ^ distance, 0, keepdims=False)

    out_mine = jnp.concatenate([head_rows(0), head_rows(2)])
    out_other = hop(jnp.concatenate([head_rows(1), head_rows(3)]), "blk", 1)
    core_out = jnp.where(
        core == 0,
        jnp.concatenate([out_mine, out_other], axis=1),
        jnp.concatenate([out_other, out_mine], axis=1),
    )

    pieces = []
    for distance in range(side):
        for away in (0, side):
            start = (blk ^ distance ^ away) * local
            pieces.append(lax.dynamic_slice_in_dim(table, start, local, 0))
    key_table = jnp.concatenate(pieces)
    row_count = x_all.shape[0]
    length = jnp.where(first, lengths[0, 0], lengths[1, 0]).astype(FULL).reshape(1, 1)
    row_valid = key_table[: 2 * local, 2 * WIDE : 2 * WIDE + 1] < length

    queries, keys, values = project(x_all, all_qkv, swap, spread, key_table[:row_count], heads)
    for bit in spread_bits:
        keys = jnp.concatenate([keys, hop(keys, "blk", bit)], axis=1)
        values = jnp.concatenate([values, hop(values, "blk", bit)], axis=1)
    attended, lse = attend(length, queries, keys, values, key_table, spread)
    chip_rows = row_count // 2
    att_other = hop(attended[chip_rows:], "blk", 2)
    att_chip = jnp.concatenate([attended[:chip_rows], att_other], axis=1)
    branch = fold_rows(mm(att_chip, core_out))
    residual_one = x_own.astype(FULL) + branch
    unit_one, scale_one = norm_parts(residual_one)
    normed = unit_one * gain_one + bias_one

    normed_low = both_rows(normed.astype(LOW))
    gate_pre = mm(normed_low, full_gate)
    up_pre = mm(normed_low, full_up)
    sigma = 1.0 / (1.0 + jnp.exp(-gate_pre))
    silu = gate_pre * sigma
    hidden = (silu * up_pre).astype(LOW)
    residual_two = normed + fold_rows(mm(hidden, full_down))
    unit_two, scale_two = norm_parts(residual_two)
    layer_rows = jnp.where(row_valid, unit_two * gain_two + bias_two, 0.0).astype(LOW)

    cot = jnp.concatenate([mine(cotangent), hop(theirs(cotangent), "blk", side)])
    upstream = jnp.where(row_valid, cot.astype(FULL), 0.0)
    grad_two, grad_gain_two, grad_bias_two = norm_back(upstream, gain_two, unit_two, scale_two)
    grad_ffn = both_rows(grad_two.astype(LOW))
    grad_down_part = mm_tn(hidden, grad_ffn).astype(LOW)
    grad_hidden = mm_nt(grad_ffn, full_down)
    grad_gate_low = (grad_hidden * up_pre * (sigma + silu * (1.0 - sigma))).astype(LOW)
    grad_up_low = (grad_hidden * silu).astype(LOW)
    grad_gate_part = mm_tn(normed_low, grad_gate_low).astype(LOW)
    grad_up_part = mm_tn(normed_low, grad_up_low).astype(LOW)
    grad_normed = grad_two + fold_rows(mm_nt(grad_gate_low, full_gate) + mm_nt(grad_up_low, full_up))
    grad_one, grad_gain_one, grad_bias_one = norm_back(grad_normed, gain_one, unit_one, scale_one)
    grad_branch = both_rows(grad_one.astype(LOW))
    grad_att = mm_nt(grad_branch, core_out).astype(LOW)
    grad_other = hop(grad_att[:, columns:], "blk", 2)
    grad_attended = jnp.concatenate([grad_att[:, :columns], grad_other])
    grad_out_part = mm_tn(att_chip, grad_branch).astype(LOW)

    grad_q, grad_k, grad_v = attend_back(length, queries, keys, values, key_table, spread, lse, grad_attended)
    for bit in reversed(spread_bits):
        half = grad_k.shape[0] // 2
        grad_k, grad_v = (
            (value[:half].astype(FULL) + hop(value[half:], "blk", bit).astype(FULL)).astype(LOW)
            for value in (grad_k, grad_v)
        )
    grad_qkv = jnp.concatenate([grad_q, grad_k, grad_v], axis=1)
    full_qkv = all_qkv.transpose(0, 2, 1, 3).reshape(width, 3 * columns)
    token_terms = mm_nt(grad_qkv, full_qkv)
    block = 2 * local
    core_sum = jnp.concatenate([token_terms[:block], token_terms[2 * block : 3 * block]]) + hop(
        jnp.concatenate([token_terms[block : 2 * block], token_terms[3 * block :]]).astype(LOW), "blk", 1
    ).astype(FULL)
    grad_rows = grad_one + core_sum[:block] + hop(core_sum[block:].astype(LOW), "blk", 2).astype(FULL)

    def send_home(rows_now):
        back = hop(rows_now[local:].astype(LOW), "blk", side).astype(rows_now.dtype)
        own = rows_now[:local]
        return jnp.where(first, jnp.stack([own, back]), jnp.stack([back, own]))[:, None]

    layer_out = send_home(layer_rows)
    grad_tokens = send_home(grad_rows)

    z_bits = bits_between(2, blk_count)

    def finish(terms):
        return sum_bits(scatter_rows(terms, dp), blk, z_bits)

    def join_columns(own):
        other = hop(own, "blk", 1)
        own, other = (v.reshape(rows, dp_count, 1, ff_half) for v in (own, other))
        joined = jnp.where(
            core == 0, jnp.concatenate([own, other], axis=2), jnp.concatenate([other, own], axis=2)
        )
        return joined.astype(FULL).reshape(rows, dp_count * 2 * ff_half)

    own_down = finish(grad_down_part.reshape(dp_count, ff_half, width))
    other_down = hop(own_down, "blk", 1)
    grad_down = jnp.where(
        core == 0, jnp.concatenate([own_down, other_down]), jnp.concatenate([other_down, own_down])
    ).astype(FULL)
    grad_gate = join_columns(finish(grad_gate_part.reshape(dp_count, rows, dp_count * ff_half)))
    grad_up = join_columns(finish(grad_up_part.reshape(dp_count, rows, dp_count * ff_half)))

    halves = grad_out_part.reshape(2 * columns, 2, half_width)
    keep_half = jnp.where(core == 0, halves[:, 0], halves[:, 1])
    send_half = jnp.where(core == 0, halves[:, 1], halves[:, 0])
    got_rows = hop(send_half, "blk", 1)
    by_part = jnp.zeros((PARTS, columns, half_width), LOW)
    for distance, value in ((0, keep_half[:columns]), (2, keep_half[columns:]), (1, got_rows[:columns]), (3, got_rows[columns:])):
        by_part = lax.dynamic_update_index_in_dim(by_part, value, part ^ distance, 0)
    sums = jnp.stack([grad_gain_one, grad_bias_one, grad_gain_two, grad_bias_two])
    sums = sums.reshape(4, dp_count, rows).transpose(1, 0, 2).reshape(dp_count, 4 * rows)
    out_terms = jnp.concatenate([by_part.reshape(dp_count, rows, half_width), pad_extra(sums.astype(LOW))], axis=1)
    own_out = finish(out_terms)
    other_out = hop(own_out, "blk", 1)
    grad_output = jnp.where(
        core == 0,
        jnp.concatenate([own_out[:rows], other_out[:rows]], axis=1),
        jnp.concatenate([other_out[:rows], own_out[:rows]], axis=1),
    ).astype(FULL)
    vector_sums = own_out[rows : rows + extra_rows].astype(FULL) + other_out[rows : rows + extra_rows].astype(FULL)
    vector_sums = vector_sums.reshape(-1)[: 4 * rows].reshape(4, rows)

    own_qkv = scatter_rows(mm_tn(x_all, grad_qkv).astype(LOW).reshape(dp_count, rows, 3 * columns), dp)
    for bit in bits_between(PARTS, blk_count):
        own_qkv = own_qkv + hop(own_qkv.astype(LOW), "blk", bit).astype(FULL)
    own_qkv = own_qkv.astype(LOW)
    near_qkv = hop(own_qkv, "blk", 2)
    pair = jnp.stack([own_qkv, near_qkv])
    other_pair = hop(pair, "blk", 1)
    by_part = jnp.zeros((PARTS, rows, 3 * columns), LOW)
    for distance, value in ((0, own_qkv), (2, near_qkv), (1, other_pair[0]), (3, other_pair[1])):
        by_part = lax.dynamic_update_index_in_dim(by_part, value, part ^ distance, 0)
    grad_query, grad_key, grad_value = (
        jnp.concatenate([by_part[t, :, m * columns : (m + 1) * columns] for t in range(PARTS)], axis=1).astype(FULL)
        for m in range(3)
    )
    return (
        layer_out, grad_tokens, grad_query, grad_key, grad_value, grad_output, grad_gate, grad_up, grad_down,
        vector_sums[0], vector_sums[1], vector_sums[2], vector_sums[3],
    )


def solution(mesh):
    slots = P(None, "dp", "blk", None)
    matrix, vector = P("dp", None), P("dp")
    return jax.shard_map(
        shards,
        mesh=mesh,
        in_specs=(slots, P(None, "dp")) + (matrix,) * 7 + (vector,) * 4 + (slots,),
        out_specs=(slots, slots) + (matrix,) * 7 + (vector,) * 4,
        check_vma=False,
    )
```

time: 1320 us -> 491 us (0.37)
  waiting for transfers between devices: 994 us -> 156 us
  matrix products: 109 us -> 40.6 us
  starting transfers between devices: 1.78 us -> 67.7 us
  blocking collectives: 42.1 us -> 0 us
  Pallas kernels: 0 us -> 39.4 us
  other arithmetic: 42.7 us -> 71.5 us
  between operations: 18 us -> 4 us
    reduce_scatter x8 -> x0, waiting for transfers between devices: 351 us -> none  [the longest x2 117 us: shards(): lax.psum_scatter(grad_up_now.astype(jnp.bfloat16), 'dp', scatter_dimensio...]
    all_gather x11 -> x0, waiting for transfers between devices: 340 us -> none  [the longest x1 54.5 us: shards(): lax.all_gather(w_up, 'dp', axis=0, tiled=True)]
    unnamed x36 -> x0, waiting for transfers between devices: 214 us -> none
    ppermute x0 -> x82, waiting for transfers between devices: none -> 156 us  [hop(): return lax.ppermute(value, axis, [(at, at ^ bit) for at in range(size)])]
    psum x1 -> x0, waiting for transfers between devices: 89.9 us -> none  [shards(): lax.psum(grad_totals[0].astype(jnp.bfloat16), 'blk').astype(jnp.float32)]
    dot_general x54 -> x14, matrix products: 109 us -> 40.6 us  [the longest x5 17.2 us: mm_nt(): lax.dot_general(left, right, (((1,), (1,)), ((), ())), preferred_element_...]
    ppermute x0 -> x82, starting transfers between devices: none -> 67.7 us  [hop(): return lax.ppermute(value, axis, [(at, at ^ bit) for at in range(size)])]
    unnamed x268 -> x158, local copies, waits for them, and re-layouts: 83.3 us -> 20.1 us
  transfers between devices with their start and end apart: 28 -> 82, of which waited for: 25 -> 30; matrix products, arithmetic and copies ran while one was open for 13% -> 35% of each run, Pallas kernels for 0% -> 8%
where the time goes in v1:
time: 491 us; the launch traced here: 485 us
  waiting for transfers between devices  156 us (32%)
  local copies, waits for them, and re-layouts  106 us (22%)
  other arithmetic  71.5 us (15%)
  starting transfers between devices  67.7 us (14%)
  matrix products  40.6 us (8%)
  Pallas kernels  39.4 us (8%)
    ppermute x82, waiting for transfers between devices, hop(): return lax.ppermute(value, axis, [(at, at ^ bit) for at in range(size)])  156 us
    ppermute x82, starting transfers between devices, hop(): return lax.ppermute(value, axis, [(at, at ^ bit) for at in range(size)])  67.7 us
    pallas_call x3, Pallas kernels, kernel_call(): pl.pallas_call(body, out_shape=outs, in_specs=in_specs, out_specs=[VMEM]...  39.4 us
    unnamed x158, local copies, waits for them, and re-layouts  20.1 us
    dot_general x5, matrix products, mm_nt(): lax.dot_general(left, right, (((1,), (1,)), ((), ())), preferred_element_...  17.2 us
    dynamic_update_slice x13, local copies, waits for them, and re-layouts, gather_rows(): out = lax.dynamic_update_index_in_dim(out, part, place ^ distance, 0)  15.1 us
    dot_general x4, matrix products, mm(): return jnp.dot(left, right, preferred_element_type=FULL)  12.3 us
    dot_general x5, matrix products, mm_tn(): lax.dot_general(left, right, (((0,), (0,)), ((), ())), preferred_element_...  11.1 us
  transfers between devices with their start and end apart: 82, of which 30 were waited for; matrix products, arithmetic and copies ran while one was open for 35% of the time, Pallas kernels for 8%

profile of v1, /device:TPU:0, one launch (start us, length us, event | category | flops | bytes accessed | tf_op | source)
XLA Modules:
  0.0 485.2 jit_solution(13779536998440272888)
XLA Ops:
  0.7 3.4 reshape.653
  4.1 2.6 fusion.88
  6.7 3.6 reshape.655
  13.8 2.9 collective-permute-start.20
  53.9 2.7 collective-permute-start
  59.4 4.7 collective-permute-done
  71.7 8.6 %collective-permute-done.12 = bf16[112,384]{1,0:T(8,128)(2,1)S(1)} collective-permute-done((bf16[112,384]{1,0:T(8,128)(2,1)S(1)}, bf16[112,384]{1,0:T(8,128)(2,1)S(1)}, u32[]{:S(2)}, u32[]{:S(2)}) %collective-permute-start.12) | collective-permute-done | bytes 86048 | tf_op jit(solution)/shard_map/ppermute | solution.py:32
  81.5 4.2 collective-permute-done.7
  112.3 6.7 %shard_map.264 = (bf16[3,1024,128]{2,1,0:T(8,128)(2,1)}, bf16[3,1024,128]{2,1,0:T(8,128)(2,1)}, bf16[3,1024,128]{2,1,0:T(8,128)(2,1)}) custom-call(bf16[1024,768]{1,0:T(8,128)(2,1)} %constant_dynamic-update-slice_fusion.x_ref, bf16[4,3,192,192]{3,2,1,0:T(8,128)(2,1)} %copy-done.2, bf16[192,384]{1,0:T(8,128)(2,1)} %constant.296.clone.swap_ref, ...), custom_call_target="tpu_custom_call" | custom-call | flops 1811939328 | bytes 6684672 | tf_op jit(solution)/shard_map/pallas_call | solution.py:163
  119.0 14.3 %shard_map.265 = (bf16[1024,192]{1,0:T(8,128)(2,1)}, f32[3,1,1024]{2,1,0:T(1,128)}) custom-call(f32[1,1]{1,0:T(1,128)} %bitcast.4.len_ref, bf16[3,1024,128]{2,1,0:T(8,128)(2,1)} %get-tuple-element.21.q_ref, bf16[3,1024,128]{2,1,0:T(8,128)(2,1)} %get-tuple-element.22.k_ref, bf16[3,1024,128]{2,1,0:T(8,128)(2,1)} %get-tuple-element.23.v_ref, ...), custom_call_target="tpu_custom_call" | custom-call | flops 1610612736 | bytes 4485124 | tf_op jit(solution)/shard_map/pallas_call | solution.py:163
  136.7 6.5 %collective-permute-done.8 = bf16[512,192]{1,0:T(8,128)(2,1)S(1)} collective-permute-done((bf16[512,192]{1,0:T(8,128)(2,1)S(1)}, bf16[512,192]{1,0:T(8,128)(2,1)S(1)}, u32[]{:S(2)}, u32[]{:S(2)}) %collective-permute-start.8) | collective-permute-done | bytes 196640 | tf_op jit(solution)/shard_map/ppermute | solution.py:32
  152.1 4.9 %collective-permute-done.27 = bf16[192,768]{1,0:T(8,128)(2,1)S(1)} collective-permute-done((bf16[192,768]{1,0:T(8,128)(2,1)}, bf16[192,768]{1,0:T(8,128)(2,1)S(1)}, u32[]{:S(2)}, u32[]{:S(2)}) %collective-permute-start.27) | collective-permute-done | bytes 294944 | tf_op jit(solution)/shard_map/ppermute | solution.py:32
  157.1 5.9 %collective-permute-done.19 = bf16[96,1536]{1,0:T(8,128)(2,1)S(1)} collective-permute-done((bf16[96,1536]{1,0:T(8,128)(2,1)S(1)}, bf16[96,1536]{1,0:T(8,128)(2,1)S(1)}, u32[]{:S(2)}, u32[]{:S(2)}) %collective-permute-start.19) | collective-permute-done | bytes 294944 | tf_op jit(solution)/shard_map/ppermute | solution.py:32
  164.8 3.2 fusion.78
  168.0 6.0 %multiply_convert_fusion.2 = (bf16[512,1536]{1,0:T(8,128)(2,1)S(1)}, f32[512,1536]{1,0:T(8,128)}) fusion(f32[512,1536]{1,0:T(8,128)S(1)} %fusion.78, bf16[768,1536]{1,0:T(8,128)(2,1)} %bitcast.28, bf16[256,768]{1,0:T(8,128)(2,1)S(1)} %collective-permute-done.15, bf16[256,768]{1,0:T(8,128)(2,1)S(1)} %fusion.11), kind=kOutput, calls=%fused_computation.5 | convolution fusion | flops 1214251008 | bytes 11010048 | tf_op jit(solution)/shard_map/dot_general | solution.py:19
  176.5 2.6 collective-permute-start.30
  181.0 7.1 %collective-permute-done.30 = bf16[128,768]{1,0:T(8,128)(2,1)S(1)} collective-permute-done((bf16[128,768]{1,0:T(8,128)(2,1)S(1)}, bf16[128,768]{1,0:T(8,128)(2,1)S(1)}, u32[]{:S(2)}, u32[]{:S(2)}) %collective-permute-start.30) | collective-permute-done | bytes 196640 | tf_op jit(solution)/shard_map/ppermute | solution.py:32
  191.8 3.3 reshape.658
  195.3 5.9 %multiply_convert_fusion.1 = (bf16[512,1536]{1,0:T(8,128)(2,1)S(1)}, bf16[512,1536]{1,0:T(8,128)(2,1)S(1)}) fusion(f32[512,1536]{1,0:T(8,128)} %get-tuple-element.135, f32[512,1536]{1,0:T(8,128)} %copy-done.70, bf16[1536,768]{1,0:T(8,128)(2,1)} %bitcast.341, bf16[256,768]{1,0:T(8,128)(2,1)} %collective-permute-done.31, bf16[256,768]{1,0:T(8,128)(2,1)} %fusion.79), kind=kOutput, calls=%fused_computation.4 | convolution fusion | flops 1218969600 | bytes 12582912 | tf_op jit(solution)/shard_map/dot_general | solution.py:23
  201.2 3.1 fusion.97
  204.3 3.2 convolution_add_fusion
  208.2 2.5 convolution_convert_fusion
  229.0 12.5 %collective-permute-done.66 = bf16[192,1536]{1,0:T(8,128)(2,1)} collective-permute-done((bf16[192,1536]{1,0:T(8,128)(2,1)}, bf16[192,1536]{1,0:T(8,128)(2,1)}, u32[]{:S(2)}, u32[]{:S(2)}) %collective-permute-start.66) | collective-permute-done | bytes 589856 | tf_op jit(solution)/shard_map/ppermute | solution.py:32
  246.1 7.1 %collective-permute-done.57 = bf16[192,1536]{1,0:T(8,128)(2,1)} collective-permute-done((bf16[192,1536]{1,0:T(8,128)(2,1)}, bf16[192,1536]{1,0:T(8,128)(2,1)}, u32[]{:S(2)}, u32[]{:S(2)}) %collective-permute-start.57) | collective-permute-done | bytes 589856 | tf_op jit(solution)/shard_map/ppermute | solution.py:32
  277.0 3.0 collective-permute-start.34
  289.6 18.4 %shard_map.266 = (bf16[1024,192]{1,0:T(8,128)(2,1)}, bf16[1024,192]{1,0:T(8,128)(2,1)}, bf16[1024,192]{1,0:T(8,128)(2,1)}) custom-call(f32[1,1]{1,0:T(1,128)} %bitcast.4.len_ref, bf16[3,1024,128]{2,1,0:T(8,128)(2,1)} %get-tuple-element.21.q_ref, bf16[3,1024,128]{2,1,0:T(8,128)(2,1)} %get-tuple-element.22.k_ref, ...), custom_call_target="tpu_custom_call" | custom-call | flops 4026531840 | bytes 5664772 | tf_op jit(solution)/shard_map/pallas_call | solution.py:163
  308.0 4.1 convolution_convert_fusion.3
  312.1 2.6 copy.74
  316.7 3.1 fusion.95
  339.7 3.9 collective-permute-done.39
  343.9 9.5 %collective-permute-done.50 = bf16[112,384]{1,0:T(8,128)(2,1)S(1)} collective-permute-done((bf16[112,384]{1,0:T(8,128)(2,1)S(1)}, bf16[112,384]{1,0:T(8,128)(2,1)S(1)}, u32[]{:S(2)}, u32[]{:S(2)}) %collective-permute-start.50) | collective-permute-done | bytes 86048 | tf_op jit(solution)/shard_map/ppermute | solution.py:32
  354.0 4.2 collective-permute-done.41
  358.3 17.6 %collective-permute-done.51 = bf16[56,384]{1,0:T(8,128)(2,1)S(1)} collective-permute-done((bf16[56,384]{1,0:T(8,128)(2,1)S(1)}, bf16[56,384]{1,0:T(8,128)(2,1)S(1)}, u32[]{:S(2)}, u32[]{:S(2)}) %collective-permute-start.51) | collective-permute-done | bytes 43040 | tf_op jit(solution)/shard_map/ppermute | solution.py:32
  375.9 3.0 collective-permute-start.52
  379.4 3.0 collective-permute-start.69
  382.5 2.8 collective-permute-done.52
  385.4 4.8 collective-permute-done.53
  390.4 17.5 %collective-permute-done.60 = bf16[48,1536]{1,0:T(8,128)(2,1)S(1)} collective-permute-done((bf16[48,1536]{1,0:T(8,128)(2,1)S(1)}, bf16[48,1536]{1,0:T(8,128)(2,1)S(1)}, u32[]{:S(2)}, u32[]{:S(2)}) %collective-permute-start.60) | collective-permute-done | bytes 147488 | tf_op jit(solution)/shard_map/ppermute | solution.py:32
  408.0 3.0 collective-permute-start.61
  412.0 8.9 %collective-permute-done.79 = bf16[96,768]{1,0:T(8,128)(2,1)S(1)} collective-permute-done((bf16[96,768]{1,0:T(8,128)(2,1)S(1)}, bf16[96,768]{1,0:T(8,128)(2,1)S(1)}, u32[]{:S(2)}, u32[]{:S(2)}) %collective-permute-start.79) | collective-permute-done | bytes 147488 | tf_op jit(solution)/shard_map/ppermute | solution.py:32
  433.6 2.8 collective-permute-done.80
  437.9 4.9 %collective-permute-done.71 = bf16[96,1536]{1,0:T(8,128)(2,1)} collective-permute-done((bf16[96,1536]{1,0:T(8,128)(2,1)S(1)}, bf16[96,1536]{1,0:T(8,128)(2,1)}, u32[]{:S(2)}, u32[]{:S(2)}) %collective-permute-start.71) | collective-permute-done | bytes 294944 | tf_op jit(solution)/shard_map/ppermute | solution.py:32
  446.7 2.3 collective-permute-done.62
  450.2 2.3 maximum_select_fusion.6
  462.5 5.1 %collective-permute-done.37 = bf16[128,768]{1,0:T(8,128)(2,1)S(1)} collective-permute-done((bf16[128,768]{1,0:T(8,128)(2,1)S(1)}, bf16[128,768]{1,0:T(8,128)(2,1)S(1)}, u32[]{:S(2)}, u32[]{:S(2)}) %collective-permute-start.37) | collective-permute-done | bytes 196640 | tf_op jit(solution)/shard_map/ppermute | solution.py:32
  472.5 2.9 reshape.685
  479.2 2.9 reshape.680
  482.2 2.9 fusion.3
  (526 shorter events, 218.4 us)
Async XLA Ops:
  13.8 74.2 %collective-permute-start.20 = (bf16[192,1536]{1,0:T(8,128)(2,1)}, bf16[192,1536]{1,0:T(8,128)(2,1)}, u32[]{:S(2)}, u32[]{:S(2)}) collective-permute-start(bf16[192,1536]{1,0:T(8,128)(2,1)} %bitcast.149), channel_id=1, source_target_pairs={{0,8},{8,0},{16,24},{24,16},{1,9},{9,1},{17,25},{25,17},{2,10},{10... | collective-permute-start | bytes 1769480 | tf_op jit(solution)/shard_map/ppermute | solution.py:32
  16.8 74.4 %collective-permute-start.21 = (bf16[192,1536]{1,0:T(8,128)(2,1)}, bf16[192,1536]{1,0:T(8,128)(2,1)}, u32[]{:S(2)}, u32[]{:S(2)}) collective-permute-start(bf16[192,1536]{1,0:T(8,128)(2,1)} %bitcast.149), channel_id=1, source_target_pairs={{0,16},{8,24},{16,0},{24,8},{1,17},{9,25},{17,1},{25,9},{2,18},{10... | collective-permute-start | bytes 1769480 | tf_op jit(solution)/shard_map/ppermute | solution.py:32
  19.9 31.6 %collective-permute-start.9 = (bf16[224,384]{1,0:T(8,128)(2,1)}, bf16[224,384]{1,0:T(8,128)(2,1)}, u32[]{:S(2)}, u32[]{:S(2)}) collective-permute-start(bf16[224,384]{1,0:T(8,128)(2,1)} %pad_maximum_fusion.29), channel_id=1, source_target_pairs={{0,8},{8,0},{16,24},{24,16},{1,9},{9,1},{17,25},{25,17},{2,10},{10... | collective-permute-start | bytes 516104 | tf_op jit(solution)/shard_map/ppermute | solution.py:32
  20.5 33.4 %collective-permute-start.10 = (bf16[224,384]{1,0:T(8,128)(2,1)}, bf16[224,384]{1,0:T(8,128)(2,1)}, u32[]{:S(2)}, u32[]{:S(2)}) collective-permute-start(bf16[224,384]{1,0:T(8,128)(2,1)} %pad_maximum_fusion.29), channel_id=1, source_target_pairs={{0,16},{8,24},{16,0},{24,8},{1,17},{9,25},{17,1},{25,9},{2,18},{10... | collective-permute-start | bytes 516104 | tf_op jit(solution)/shard_map/ppermute | solution.py:32
  23.4 42.7 %collective-permute-start.4 = (bf16[3,192,192]{2,1,0:T(8,128)(2,1)}, bf16[3,192,192]{2,1,0:T(8,128)(2,1)}, u32[]{:S(2)}, u32[]{:S(2)}) collective-permute-start(bf16[3,192,192]{2,1,0:T(8,128)(2,1)} %pad_maximum_fusion.23), channel_id=1, source_target_pairs={{0,8},{8,0},{16,24},{24,16},{1,9},{9,1},{17,25},{25,17},{2,10},{10... | collective-permute-start | bytes 663560 | tf_op jit(solution)/shard_map/ppermute | solution.py:32
  51.5 16.1 %collective-permute-start.5 = (bf16[3,192,192]{2,1,0:T(8,128)(2,1)}, bf16[3,192,192]{2,1,0:T(8,128)(2,1)S(1)}, u32[]{:S(2)}, u32[]{:S(2)}) collective-permute-start(bf16[3,192,192]{2,1,0:T(8,128)(2,1)} %pad_maximum_fusion.23), channel_id=1, source_target_pairs={{0,16},{8,24},{16,0},{24,8},{1,17},{9,25},{17,1},{25,9},{2,18},{10... | collective-permute-start | bytes 663560 | tf_op jit(solution)/shard_map/ppermute | solution.py:32
  64.1 29.4 %collective-permute-start.16 = (bf16[192,1536]{1,0:T(8,128)(2,1)}, bf16[192,1536]{1,0:T(8,128)(2,1)S(1)}, u32[]{:S(2)}, u32[]{:S(2)}) collective-permute-start(bf16[192,1536]{1,0:T(8,128)(2,1)} %bitcast.144), channel_id=1, source_target_pairs={{0,8},{8,0},{16,24},{24,16},{1,9},{9,1},{17,25},{25,17},{2,10},{10... | collective-permute-start | bytes 1769480 | tf_op jit(solution)/shard_map/ppermute | solution.py:32
  91.2 18.6 %collective-permute-start.25 = (bf16[384,768]{1,0:T(8,128)(2,1)}, bf16[384,768]{1,0:T(8,128)(2,1)S(1)}, u32[]{:S(2)}, u32[]{:S(2)}) collective-permute-start(bf16[384,768]{1,0:T(8,128)(2,1)} %get-tuple-element.49), channel_id=1, source_target_pairs={{0,16},{8,24},{16,0},{24,8},{1,17},{9,25},{17,1},{25,9},{2,18},{10... | collective-permute-start | bytes 1769480 | tf_op jit(solution)/shard_map/ppermute | solution.py:32
  94.9 40.6 %collective-permute-start.13 = (bf16[384,384]{1,0:T(8,128)(2,1)}, bf16[384,384]{1,0:T(8,128)(2,1)}, u32[]{:S(2)}, u32[]{:S(2)}) collective-permute-start(bf16[384,384]{1,0:T(8,128)(2,1)} %pad_maximum_fusion.24), channel_id=1, source_target_pairs={{0,1},{1,0},{2,3},{3,2},{4,5},{5,4},{6,7},{7,6},{8,9},{9,8},{10,11... | collective-permute-start | bytes 884744 | tf_op jit(solution)/shard_map/ppermute | solution.py:32
  98.2 50.9 %collective-permute-start.22 = (bf16[96,1536]{1,0:T(8,128)(2,1)}, bf16[96,1536]{1,0:T(8,128)(2,1)}, u32[]{:S(2)}, u32[]{:S(2)}) collective-permute-start(bf16[96,1536]{1,0:T(8,128)(2,1)} %slice.660), channel_id=1, source_target_pairs={{0,16},{8,24},{16,0},{24,8},{1,17},{9,25},{17,1},{25,9},{2,18},{10... | collective-permute-start | bytes 884744 | tf_op jit(solution)/shard_map/ppermute | solution.py:32
  102.5 47.7 %collective-permute-start.23 = (bf16[96,1536]{1,0:T(8,128)(2,1)}, bf16[96,1536]{1,0:T(8,128)(2,1)}, u32[]{:S(2)}, u32[]{:S(2)}) collective-permute-start(bf16[96,1536]{1,0:T(8,128)(2,1)} %slice.661), channel_id=1, source_target_pairs={{0,8},{8,0},{16,24},{24,16},{1,9},{9,1},{17,25},{25,17},{2,10},{10... | collective-permute-start | bytes 884744 | tf_op jit(solution)/shard_map/ppermute | solution.py:32
  105.8 51.3 %collective-permute-start.18 = (bf16[96,1536]{1,0:T(8,128)(2,1)}, bf16[96,1536]{1,0:T(8,128)(2,1)}, u32[]{:S(2)}, u32[]{:S(2)}) collective-permute-start(bf16[96,1536]{1,0:T(8,128)(2,1)} %slice.656), channel_id=1, source_target_pairs={{0,16},{8,24},{16,0},{24,8},{1,17},{9,25},{17,1},{25,9},{2,18},{10... | collective-permute-start | bytes 884744 | tf_op jit(solution)/shard_map/ppermute | solution.py:32
  135.5 16.6 %collective-permute-start.26 = (bf16[192,768]{1,0:T(8,128)(2,1)S(1)}, bf16[192,768]{1,0:T(8,128)(2,1)S(1)}, u32[]{:S(2)}, u32[]{:S(2)}) collective-permute-start(bf16[192,768]{1,0:T(8,128)(2,1)S(1)} %copy-done.47), channel_id=1, source_target_pairs={{0,16},{8,24},{16,0},{24,8},{1,17},{9,25},{17,1},{25,9},{2,18},{10... | collective-permute-start | bytes 884744 | tf_op jit(solution)/shard_map/ppermute | solution.py:32
  150.2 14.5 %collective-permute-start.15 = (bf16[256,768]{1,0:T(8,128)(2,1)S(1)}, bf16[256,768]{1,0:T(8,128)(2,1)S(1)}, u32[]{:S(2)}, u32[]{:S(2)}) collective-permute-start(bf16[256,768]{1,0:T(8,128)(2,1)S(1)} %fusion.11), channel_id=1, source_target_pairs={{0,1},{1,0},{2,3},{3,2},{4,5},{5,4},{6,7},{7,6},{8,9},{9,8},{10,11... | collective-permute-start | bytes 1179656 | tf_op jit(solution)/shard_map/ppermute | solution.py:32
  207.6 17.4 %collective-permute-start.32 = (bf16[256,768]{1,0:T(8,128)(2,1)S(1)}, bf16[256,768]{1,0:T(8,128)(2,1)S(1)}, u32[]{:S(2)}, u32[]{:S(2)}) collective-permute-start(bf16[256,768]{1,0:T(8,128)(2,1)S(1)} %slice.869), channel_id=1, source_target_pairs={{0,1},{1,0},{2,3},{3,2},{4,5},{5,4},{6,7},{7,6},{8,9},{9,8},{10,11... | collective-permute-start | bytes 1179656 | tf_op jit(solution)/shard_map/ppermute | solution.py:32
  212.3 44.0 %collective-permute-start.75 = (bf16[384,768]{1,0:T(8,128)(2,1)}, bf16[384,768]{1,0:T(8,128)(2,1)}, u32[]{:S(2)}, u32[]{:S(2)}) collective-permute-start(bf16[384,768]{1,0:T(8,128)(2,1)} %pad_maximum_fusion.10), channel_id=1, source_target_pairs={{0,16},{8,24},{16,0},{24,8},{1,17},{9,25},{17,1},{25,9},{2,18},{10... | collective-permute-start | bytes 1769480 | tf_op jit(solution)/shard_map/ppermute | solution.py:32
  214.6 44.9 %collective-permute-start.73 = (bf16[384,768]{1,0:T(8,128)(2,1)}, bf16[384,768]{1,0:T(8,128)(2,1)}, u32[]{:S(2)}, u32[]{:S(2)}) collective-permute-start(bf16[384,768]{1,0:T(8,128)(2,1)} %pad_maximum_fusion.9), channel_id=1, source_target_pairs={{0,8},{8,0},{16,24},{24,16},{1,9},{9,1},{17,25},{25,17},{2,10},{10... | collective-permute-start | bytes 1769480 | tf_op jit(solution)/shard_map/ppermute | solution.py:32
  218.3 23.2 %collective-permute-start.66 = (bf16[192,1536]{1,0:T(8,128)(2,1)}, bf16[192,1536]{1,0:T(8,128)(2,1)}, u32[]{:S(2)}, u32[]{:S(2)}) collective-permute-start(bf16[192,1536]{1,0:T(8,128)(2,1)} %pad_maximum_fusion.8), channel_id=1, source_target_pairs={{0,16},{8,24},{16,0},{24,8},{1,17},{9,25},{17,1},{25,9},{2,18},{10... | collective-permute-start | bytes 1769480 | tf_op jit(solution)/shard_map/ppermute | solution.py:32
  220.6 41.5 %collective-permute-start.64 = (bf16[192,1536]{1,0:T(8,128)(2,1)}, bf16[192,1536]{1,0:T(8,128)(2,1)}, u32[]{:S(2)}, u32[]{:S(2)}) collective-permute-start(bf16[192,1536]{1,0:T(8,128)(2,1)} %pad_maximum_fusion.7), channel_id=1, source_target_pairs={{0,8},{8,0},{16,24},{24,16},{1,9},{9,1},{17,25},{25,17},{2,10},{10... | collective-permute-start | bytes 1769480 | tf_op jit(solution)/shard_map/ppermute | solution.py:32
  225.0 28.2 %collective-permute-start.57 = (bf16[192,1536]{1,0:T(8,128)(2,1)}, bf16[192,1536]{1,0:T(8,128)(2,1)}, u32[]{:S(2)}, u32[]{:S(2)}) collective-permute-start(bf16[192,1536]{1,0:T(8,128)(2,1)} %pad_maximum_fusion.6), channel_id=1, source_target_pairs={{0,16},{8,24},{16,0},{24,8},{1,17},{9,25},{17,1},{25,9},{2,18},{10... | collective-permute-start | bytes 1769480 | tf_op jit(solution)/shard_map/ppermute | solution.py:32
  241.5 23.5 %collective-permute-start.55 = (bf16[192,1536]{1,0:T(8,128)(2,1)S(1)}, bf16[192,1536]{1,0:T(8,128)(2,1)S(1)}, u32[]{:S(2)}, u32[]{:S(2)}) collective-permute-start(bf16[192,1536]{1,0:T(8,128)(2,1)S(1)} %copy-done.41), channel_id=1, source_target_pairs={{0,8},{8,0},{16,24},{24,16},{1,9},{9,1},{17,25},{25,17},{2,10},{10... | collective-permute-start | bytes 1769480 | tf_op jit(solution)/shard_map/ppermute | solution.py:32
  253.2 16.4 %collective-permute-start.33 = (bf16[256,768]{1,0:T(8,128)(2,1)}, bf16[256,768]{1,0:T(8,128)(2,1)S(1)}, u32[]{:S(2)}, u32[]{:S(2)}) collective-permute-start(bf16[256,768]{1,0:T(8,128)(2,1)} %get-tuple-element.43), channel_id=1, source_target_pairs={{0,1},{1,0},{2,3},{3,2},{4,5},{5,4},{6,7},{7,6},{8,9},{9,8},{10,11... | collective-permute-start | bytes 1179656 | tf_op jit(solution)/shard_map/ppermute | solution.py:32
  259.5 20.5 %collective-permute-start.76 = (bf16[192,768]{1,0:T(8,128)(2,1)}, bf16[192,768]{1,0:T(8,128)(2,1)}, u32[]{:S(2)}, u32[]{:S(2)}) collective-permute-start(bf16[192,768]{1,0:T(8,128)(2,1)} %fusion.24), channel_id=1, source_target_pairs={{0,8},{8,0},{16,24},{24,16},{1,9},{9,1},{17,25},{25,17},{2,10},{10... | collective-permute-start | bytes 884744 | tf_op jit(solution)/shard_map/ppermute | solution.py:32
  262.1 20.5 %collective-permute-start.67 = (bf16[96,1536]{1,0:T(8,128)(2,1)}, bf16[96,1536]{1,0:T(8,128)(2,1)}, u32[]{:S(2)}, u32[]{:S(2)}) collective-permute-start(bf16[96,1536]{1,0:T(8,128)(2,1)} %fusion.28), channel_id=1, source_target_pairs={{0,8},{8,0},{16,24},{24,16},{1,9},{9,1},{17,25},{25,17},{2,10},{10... | collective-permute-start | bytes 884744 | tf_op jit(solution)/shard_map/ppermute | solution.py:32
  265.0 21.1 %collective-permute-start.58 = (bf16[96,1536]{1,0:T(8,128)(2,1)}, bf16[96,1536]{1,0:T(8,128)(2,1)}, u32[]{:S(2)}, u32[]{:S(2)}) collective-permute-start(bf16[96,1536]{1,0:T(8,128)(2,1)} %fusion.32), channel_id=1, source_target_pairs={{0,8},{8,0},{16,24},{24,16},{1,9},{9,1},{17,25},{25,17},{2,10},{10... | collective-permute-start | bytes 884744 | tf_op jit(solution)/shard_map/ppermute | solution.py:32
  274.9 45.2 %collective-permute-start.45 = (bf16[384,384]{1,0:T(8,128)(2,1)}, bf16[384,384]{1,0:T(8,128)(2,1)}, u32[]{:S(2)}, u32[]{:S(2)}) collective-permute-start(bf16[384,384]{1,0:T(8,128)(2,1)} %get-tuple-element.81), channel_id=1, source_target_pairs={{0,1},{1,0},{2,3},{3,2},{4,5},{5,4},{6,7},{7,6},{8,9},{9,8},{10,11... | collective-permute-start | bytes 884744 | tf_op jit(solution)/shard_map/ppermute | solution.py:32
  282.0 43.0 %collective-permute-start.74 = (bf16[192,768]{1,0:T(8,128)(2,1)}, bf16[192,768]{1,0:T(8,128)(2,1)}, u32[]{:S(2)}, u32[]{:S(2)}) collective-permute-start(bf16[192,768]{1,0:T(8,128)(2,1)} %get-tuple-element.59), channel_id=1, source_target_pairs={{0,16},{8,24},{16,0},{24,8},{1,17},{9,25},{17,1},{25,9},{2,18},{10... | collective-permute-start | bytes 884744 | tf_op jit(solution)/shard_map/ppermute | solution.py:32
  284.7 38.9 %collective-permute-start.65 = (bf16[96,1536]{1,0:T(8,128)(2,1)}, bf16[96,1536]{1,0:T(8,128)(2,1)}, u32[]{:S(2)}, u32[]{:S(2)}) collective-permute-start(bf16[96,1536]{1,0:T(8,128)(2,1)} %get-tuple-element.65), channel_id=1, source_target_pairs={{0,16},{8,24},{16,0},{24,8},{1,17},{9,25},{17,1},{25,9},{2,18},{10... | collective-permute-start | bytes 884744 | tf_op jit(solution)/shard_map/ppermute | solution.py:32
  288.1 39.5 %collective-permute-start.56 = (bf16[96,1536]{1,0:T(8,128)(2,1)}, bf16[96,1536]{1,0:T(8,128)(2,1)}, u32[]{:S(2)}, u32[]{:S(2)}) collective-permute-start(bf16[96,1536]{1,0:T(8,128)(2,1)} %get-tuple-element.71), channel_id=1, source_target_pairs={{0,16},{8,24},{16,0},{24,8},{1,17},{9,25},{17,1},{25,9},{2,18},{10... | collective-permute-start | bytes 884744 | tf_op jit(solution)/shard_map/ppermute | solution.py:32
  320.1 14.8 %collective-permute-start.40 = (bf16[192,576]{1,0:T(8,128)(2,1)S(1)}, bf16[192,576]{1,0:T(8,128)(2,1)S(1)}, u32[]{:S(2)}, u32[]{:S(2)}) collective-permute-start(bf16[192,576]{1,0:T(8,128)(2,1)S(1)} %pad_maximum_fusion.26), channel_id=1, source_target_pairs={{0,16},{8,24},{16,0},{24,8},{1,17},{9,25},{17,1},{25,9},{2,18},{10... | collective-permute-start | bytes 663560 | tf_op jit(solution)/shard_map/ppermute | solution.py:32
  323.6 101.3 %collective-permute-start.35 = (bf16[512,768]{1,0:T(8,128)(2,1)S(1)}, bf16[512,768]{1,0:T(8,128)(2,1)S(1)}, u32[]{:S(2)}, u32[]{:S(2)}) collective-permute-start(bf16[512,768]{1,0:T(8,128)(2,1)S(1)} %pad_maximum_fusion.4), channel_id=1, source_target_pairs={{0,1},{1,0},{2,3},{3,2},{4,5},{5,4},{6,7},{7,6},{8,9},{9,8},{10,11... | collective-permute-start | bytes 2359304 | tf_op jit(solution)/shard_map/ppermute | solution.py:32
  329.9 46.0 %collective-permute-start.77 = (bf16[192,768]{1,0:T(8,128)(2,1)S(1)}, bf16[192,768]{1,0:T(8,128)(2,1)S(1)}, u32[]{:S(2)}, u32[]{:S(2)}) collective-permute-start(bf16[192,768]{1,0:T(8,128)(2,1)S(1)} %fusion.13), channel_id=1, source_target_pairs={{0,2},{1,3},{2,0},{3,1},{4,6},{5,7},{6,4},{7,5},{8,10},{9,11},{10,... | collective-permute-start | bytes 884744 | tf_op jit(solution)/shard_map/ppermute | solution.py:32
  334.9 44.2 %collective-permute-start.68 = (bf16[96,1536]{1,0:T(8,128)(2,1)S(1)}, bf16[96,1536]{1,0:T(8,128)(2,1)S(1)}, u32[]{:S(2)}, u32[]{:S(2)}) collective-permute-start(bf16[96,1536]{1,0:T(8,128)(2,1)S(1)} %fusion.17), channel_id=1, source_target_pairs={{0,2},{1,3},{2,0},{3,1},{4,6},{5,7},{6,4},{7,5},{8,10},{9,11},{10,... | collective-permute-start | bytes 884744 | tf_op jit(solution)/shard_map/ppermute | solution.py:32
  336.4 43.0 %collective-permute-start.59 = (bf16[96,1536]{1,0:T(8,128)(2,1)S(1)}, bf16[96,1536]{1,0:T(8,128)(2,1)S(1)}, u32[]{:S(2)}, u32[]{:S(2)}) collective-permute-start(bf16[96,1536]{1,0:T(8,128)(2,1)S(1)} %fusion.21), channel_id=1, source_target_pairs={{0,2},{1,3},{2,0},{3,1},{4,6},{5,7},{6,4},{7,5},{8,10},{9,11},{10,... | collective-permute-start | bytes 884744 | tf_op jit(solution)/shard_map/ppermute | solution.py:32
  358.2 17.7 %collective-permute-start.51 = (bf16[56,384]{1,0:T(8,128)(2,1)S(1)}, bf16[56,384]{1,0:T(8,128)(2,1)S(1)}, u32[]{:S(2)}, u32[]{:S(2)}) collective-permute-start(bf16[56,384]{1,0:T(8,128)(2,1)S(1)} %dynamic-slice_convert_fusion.3), channel_id=1, source_target_pairs={{0,4},{1,5},{2,6},{3,7},{4,0},{5,1},{6,2},{7,3},{8,12},{9,13},{10,... | collective-permute-start | bytes 129032 | tf_op jit(solution)/shard_map/ppermute | solution.py:32
  375.9 35.1 %collective-permute-start.42 = (bf16[192,576]{1,0:T(8,128)(2,1)S(1)}, bf16[192,576]{1,0:T(8,128)(2,1)S(1)}, u32[]{:S(2)}, u32[]{:S(2)}) collective-permute-start(bf16[192,576]{1,0:T(8,128)(2,1)S(1)} %fusion.40), channel_id=1, source_target_pairs={{0,4},{1,5},{2,6},{3,7},{4,0},{5,1},{6,2},{7,3},{8,12},{9,13},{10,... | collective-permute-start | bytes 663560 | tf_op jit(solution)/shard_map/ppermute | solution.py:32
  379.1 28.9 %collective-permute-start.78 = (bf16[96,768]{1,0:T(8,128)(2,1)S(1)}, bf16[96,768]{1,0:T(8,128)(2,1)S(1)}, u32[]{:S(2)}, u32[]{:S(2)}) collective-permute-start(bf16[96,768]{1,0:T(8,128)(2,1)S(1)} %dynamic-slice_convert_fusion), channel_id=1, source_target_pairs={{0,4},{1,5},{2,6},{3,7},{4,0},{5,1},{6,2},{7,3},{8,12},{9,13},{10,... | collective-permute-start | bytes 442376 | tf_op jit(solution)/shard_map/ppermute | solution.py:32
  390.2 17.7 %collective-permute-start.60 = (bf16[48,1536]{1,0:T(8,128)(2,1)S(1)}, bf16[48,1536]{1,0:T(8,128)(2,1)S(1)}, u32[]{:S(2)}, u32[]{:S(2)}) collective-permute-start(bf16[48,1536]{1,0:T(8,128)(2,1)S(1)} %dynamic-slice_convert_fusion.2), channel_id=1, source_target_pairs={{0,4},{1,5},{2,6},{3,7},{4,0},{5,1},{6,2},{7,3},{8,12},{9,13},{10,... | collective-permute-start | bytes 442376 | tf_op jit(solution)/shard_map/ppermute | solution.py:32
  390.3 38.4 %collective-permute-start.54 = (bf16[224,384]{1,0:T(8,128)(2,1)S(1)}, bf16[224,384]{1,0:T(8,128)(2,1)S(1)}, u32[]{:S(2)}, u32[]{:S(2)}) collective-permute-start(bf16[224,384]{1,0:T(8,128)(2,1)S(1)} %maximum_select_fusion.17), channel_id=1, source_target_pairs={{0,1},{1,0},{2,3},{3,2},{4,5},{5,4},{6,7},{7,6},{8,9},{9,8},{10,11... | collective-permute-start | bytes 516104 | tf_op jit(solution)/shard_map/ppermute | solution.py:32
  408.0 15.2 %collective-permute-start.61 = (bf16[48,1536]{1,0:T(8,128)(2,1)S(1)}, bf16[48,1536]{1,0:T(8,128)(2,1)S(1)}, u32[]{:S(2)}, u32[]{:S(2)}) collective-permute-start(bf16[48,1536]{1,0:T(8,128)(2,1)S(1)} %add_convert_fusion.3), channel_id=1, source_target_pairs={{0,4},{1,5},{2,6},{3,7},{4,0},{5,1},{6,2},{7,3},{8,12},{9,13},{10,... | collective-permute-start | bytes 442376 | tf_op jit(solution)/shard_map/ppermute | solution.py:32
  421.0 15.4 %collective-permute-start.80 = (bf16[192,768]{1,0:T(8,128)(2,1)S(1)}, bf16[192,768]{1,0:T(8,128)(2,1)}, u32[]{:S(2)}, u32[]{:S(2)}) collective-permute-start(bf16[192,768]{1,0:T(8,128)(2,1)S(1)} %maximum_select_fusion.16), channel_id=1, source_target_pairs={{0,2},{1,3},{2,0},{3,1},{4,6},{5,7},{6,4},{7,5},{8,10},{9,11},{10,... | collective-permute-start | bytes 884744 | tf_op jit(solution)/shard_map/ppermute | solution.py:32
  423.2 19.6 %collective-permute-start.71 = (bf16[96,1536]{1,0:T(8,128)(2,1)S(1)}, bf16[96,1536]{1,0:T(8,128)(2,1)}, u32[]{:S(2)}, u32[]{:S(2)}) collective-permute-start(bf16[96,1536]{1,0:T(8,128)(2,1)S(1)} %maximum_select_fusion.14), channel_id=1, source_target_pairs={{0,2},{1,3},{2,0},{3,1},{4,6},{5,7},{6,4},{7,5},{8,10},{9,11},{10,... | collective-permute-start | bytes 884744 | tf_op jit(solution)/shard_map/ppermute | solution.py:32
  424.8 24.2 %collective-permute-start.62 = (bf16[96,1536]{1,0:T(8,128)(2,1)}, bf16[96,1536]{1,0:T(8,128)(2,1)}, u32[]{:S(2)}, u32[]{:S(2)}) collective-permute-start(bf16[96,1536]{1,0:T(8,128)(2,1)} %maximum_select_fusion.12), channel_id=1, source_target_pairs={{0,2},{1,3},{2,0},{3,1},{4,6},{5,7},{6,4},{7,5},{8,10},{9,11},{10,... | collective-permute-start | bytes 884744 | tf_op jit(solution)/shard_map/ppermute | solution.py:32
  428.6 27.0 %collective-permute-start.36 = (bf16[256,768]{1,0:T(8,128)(2,1)}, bf16[256,768]{1,0:T(8,128)(2,1)}, u32[]{:S(2)}, u32[]{:S(2)}) collective-permute-start(bf16[256,768]{1,0:T(8,128)(2,1)} %slice.868), channel_id=1, source_target_pairs={{0,2},{1,3},{2,0},{3,1},{4,6},{5,7},{6,4},{7,5},{8,10},{9,11},{10,... | collective-permute-start | bytes 1179656 | tf_op jit(solution)/shard_map/ppermute | solution.py:32
  433.6 23.9 %collective-permute-start.44 = (bf16[2,192,576]{2,1,0:T(8,128)(2,1)}, bf16[2,192,576]{2,1,0:T(8,128)(2,1)}, u32[]{:S(2)}, u32[]{:S(2)}) collective-permute-start(bf16[2,192,576]{2,1,0:T(8,128)(2,1)} %pad_maximum_fusion.17), channel_id=1, source_target_pairs={{0,1},{1,0},{2,3},{3,2},{4,5},{5,4},{6,7},{7,6},{8,9},{9,8},{10,11... | collective-permute-start | bytes 1327112 | tf_op jit(solution)/shard_map/ppermute | solution.py:32
  437.8 44.4 %collective-permute-start.81 = (bf16[384,768]{1,0:T(8,128)(2,1)S(1)}, bf16[384,768]{1,0:T(8,128)(2,1)}, u32[]{:S(2)}, u32[]{:S(2)}) collective-permute-start(bf16[384,768]{1,0:T(8,128)(2,1)S(1)} %maximum_select_fusion.9), channel_id=1, source_target_pairs={{0,1},{1,0},{2,3},{3,2},{4,5},{5,4},{6,7},{7,6},{8,9},{9,8},{10,11... | collective-permute-start | bytes 1769480 | tf_op jit(solution)/shard_map/ppermute | solution.py:32
  446.7 21.9 %collective-permute-start.72 = (bf16[192,1536]{1,0:T(8,128)(2,1)}, bf16[192,1536]{1,0:T(8,128)(2,1)}, u32[]{:S(2)}, u32[]{:S(2)}) collective-permute-start(bf16[192,1536]{1,0:T(8,128)(2,1)} %maximum_select_fusion.8), channel_id=1, source_target_pairs={{0,1},{1,0},{2,3},{3,2},{4,5},{5,4},{6,7},{7,6},{8,9},{9,8},{10,11... | collective-permute-start | bytes 1769480 | tf_op jit(solution)/shard_map/ppermute | solution.py:32
  452.5 23.0 %collective-permute-start.63 = (bf16[192,1536]{1,0:T(8,128)(2,1)}, bf16[192,1536]{1,0:T(8,128)(2,1)}, u32[]{:S(2)}, u32[]{:S(2)}) collective-permute-start(bf16[192,1536]{1,0:T(8,128)(2,1)} %maximum_select_fusion.6), channel_id=1, source_target_pairs={{0,1},{1,0},{2,3},{3,2},{4,5},{5,4},{6,7},{7,6},{8,9},{9,8},{10,11... | collective-permute-start | bytes 1769480 | tf_op jit(solution)/shard_map/ppermute | solution.py:32
  (107 other events, 717.5 us)
